TPU v7x, 256 devices: a whole 4x4x8 slice. The times are simulated.
256 devices in a mesh: shot: 16 (over y, z_lo, core), dom: 16 (over z_hi, x).
Axes of the slice: x: 4, y: 4, z: 8 (z_hi: 4, z_lo: 2; z = z_hi * 2 + z_lo), core: 2. Of those that a mesh axis runs over, the one named last changes fastest.
Arguments:
- velocity_term: float32 [128, 8, 2048], P('dom'), may hold values from 0.05 to 0.3
- wave_prev: float32 [64, 128, 8, 2048], P('shot', 'dom'), may hold values from -6 to 6
- wave_now: float32 [64, 128, 8, 2048], P('shot', 'dom'), may hold values from -6 to 6
- adjoint_next: float32 [64, 128, 8, 2048], P('shot', 'dom'), may hold values from -6 to 6
- adjoint_now: float32 [64, 128, 8, 2048], P('shot', 'dom'), may hold values from -6 to 6
- source_cell: int32 [64], P('shot'), may hold values from 0 to 2097151
- source_wave: float32 [64, 2], P('shot'), may hold values from -16 to 16
- receiver_cells: int32 [64, 256], P('shot'), may hold values from 0 to 2097151
- data_residual: float32 [64, 2, 256], P('shot'), may hold values from -6 to 6
- aperture: int32 [64, 8], P('shot'), may hold values from 0 to 15, all different within a row
Outputs:
- gradient: float32 [128, 8, 2048], P('dom')
Inputs may be any that keep to these rules, and one draw needn't show every extreme that they name: `aperture`: each row names 8 different domain blocks, and every block is named by some shot.
All inputs are finite; a program needn't handle non-finite values.
Results may differ from a plain program's by a relative error of at most 0.0003.
Values sent between devices are 32-bit elements; how exact they have to be, the bound alone decides.
A program may use at most 128 MiB of HBM per device.

v0:
```python
import jax
import jax.numpy as jnp
from jax import lax
from jax.sharding import PartitionSpec as P


def extended(cells, sides, width):
    for axis, dim in sides:
        count = lax.axis_size(axis)
        ends = count - 1
        head = lax.slice_in_dim(cells, 0, width, axis=dim)
        tail = lax.slice_in_dim(cells, cells.shape[dim] - width, cells.shape[dim], axis=dim)
        cells = jnp.concatenate(
            [
                lax.ppermute(tail, axis, [(i, (i + 1) % count) for i in range(ends)]),
                cells,
                lax.ppermute(head, axis, [((i + 1) % count, i) for i in range(ends)]),
            ],
            axis=dim,
        )
    return cells


def laplace(padded):
    inner = padded[:, 1:-1]
    side = jnp.pad(inner, ((0, 0), (0, 0), (1, 1), (1, 1)))
    beside = padded[:, 2:] + padded[:, :-2]
    beside = beside + side[:, :, 2:, 1:-1] + side[:, :, :-2, 1:-1]
    beside = beside + side[:, :, 1:-1, 2:] + side[:, :, 1:-1, :-2]
    return beside - 6.0 * inner


def inject(field, cells, values, offset):
    shots = field.shape[0]
    volume = field.shape[1] * field.shape[2] * field.shape[3]
    local = cells - offset
    valid = (local >= 0) & (local < volume)
    target = jnp.where(valid, local, volume)
    shot_rows = jnp.broadcast_to(jnp.arange(shots, dtype=jnp.int32)[:, None], target.shape)
    flat = field.reshape(shots, volume).at[shot_rows, target].add(values, mode="drop")
    return flat.reshape(field.shape)


def wave_halo(field):
    return extended(field, (("dom", 1),), 1)


def adjoint_halo(field):
    return extended(field, (("dom", 1),), 1)


def body(
    velocity_term,
    wave_prev,
    wave_now,
    adjoint_next,
    adjoint_now,
    source_cell,
    source_wave,
    receiver_cells,
    data_residual,
    aperture,
):
    shots, width, levels, columns = wave_now.shape
    plane = levels * columns
    offset = lax.axis_index("dom") * (width * plane)
    source_cells = source_cell[:, None]

    def advance(now, before, padded, cells, values):
        return inject(2.0 * now - before + velocity_term * laplace(padded), cells, values, offset)

    wave_one = advance(wave_now, wave_prev, wave_halo(wave_now), source_cells, source_wave[:, 0:1])
    wave_two = advance(wave_one, wave_now, wave_halo(wave_one), source_cells, source_wave[:, 1:2])
    adjoint_one = advance(
        adjoint_now, adjoint_next, adjoint_halo(adjoint_now), receiver_cells, data_residual[:, 0]
    )
    adjoint_zero = advance(
        adjoint_one, adjoint_now, adjoint_halo(adjoint_one), receiver_cells, data_residual[:, 1]
    )
    image = adjoint_one * (wave_two - 2.0 * wave_one + wave_now) + adjoint_zero * (
        wave_one - 2.0 * wave_now + wave_prev
    )
    inside = jnp.any(aperture == lax.axis_index("dom"), axis=1).astype(jnp.float32)
    partial_image = jnp.sum(image * inside[:, None, None, None], axis=0)
    total = lax.psum(partial_image, "shot")
    return total * float(lax.axis_size("shot") * shots) ** (-0.5)


def solution(mesh):
    placed = (
        P("dom", None, None),
        P("shot", "dom", None, None),
        P("shot", "dom", None, None),
        P("shot", "dom", None, None),
        P("shot", "dom", None, None),
        P("shot"),
        P("shot", None),
        P("shot", None),
        P("shot", None, None),
        P("shot", None),
    )
    return jax.shard_map(
        body, mesh=mesh, in_specs=placed, out_specs=P("dom", None, None), check_vma=False
    )
```

profile of v0, /device:TPU:65, one launch (start us, length us, event | category | flops | bytes accessed | tf_op | source)
XLA Modules:
  0.0 259.7 jit_solution(9231765566176760570)
XLA Ops:
  6.6 0.0 all-reduce.6.cloned.1.call-start
  6.6 2.0 fusion.46
  8.6 3.5 %collective-permute-start = (f32[4,1,8,2048]{3,2,1,0:T(8,128)}, f32[4,1,8,2048]{3,2,1,0:T(8,128)S(1)}, u32[]{:S(2)}, u32[]{:S(2)}) collective-permute-start(f32[4,1,8,2048]{3,2,1,0:T(8,128)} %get-tuple-element.11), channel_id=1, source_target_pairs={{1,0},{2,1},{3,2},{4,3},{5,4},{6,5},{7,6},{8,7},{9,8},{10,9},{11,1... | collective-permute-start | bytes 786440 | tf_op jit(solution)/shard_map/ppermute | solution.py:17
  12.1 1.9 collective-permute-start.1
  14.0 1.8 fusion.45
  15.8 6.4 %collective-permute-start.2 = (f32[4,1,8,2048]{3,2,1,0:T(8,128)}, f32[4,1,8,2048]{3,2,1,0:T(8,128)S(1)}, u32[]{:S(2)}, u32[]{:S(2)}) collective-permute-start(f32[4,1,8,2048]{3,2,1,0:T(8,128)} %get-tuple-element.9), channel_id=1, source_target_pairs={{1,0},{2,1},{3,2},{4,3},{5,4},{6,5},{7,6},{8,7},{9,8},{10,9},{11,1... | collective-permute-start | bytes 786440 | tf_op jit(solution)/shard_map/ppermute | solution.py:17
  22.1 1.9 collective-permute-start.3
  24.1 0.0 copy-done.7
  24.1 0.1 and_reduce_fusion
  24.2 0.1 multiply_reduce_fusion
  24.4 0.0 collective-permute-done
  24.4 0.0 collective-permute-done.1
  24.4 3.0 %fusion.6 = f32[4,8,8,2048]{3,2,1,0:T(8,128)S(1)} fusion(f32[4,8,8,2048]{3,2,1,0:T(8,128)S(1)} %copy-done.2, f32[4,1,8,2048]{3,2,1,0:T(8,128)S(1)} %collective-permute-done.1, f32[4,1,8,2048]{3,2,1,0:T(8,128)S(1)} %collective-permute-done, f32[4,8,8,2048]{3,2,1,0:T(8,128)} %param.13, f32[8,8,2048]{2,1,0:T(8,128)} %param.10), kind=kLoop, calls=%fused_computation.26 | loop fusion | flops 6815744 | bytes 7340032 | tf_op jit(solution)/shard_map/add | solution.py:70
  27.4 0.4 copy.11
  27.8 6.8 %scatter_fusion.2 = f32[524288]{0:T(1024)S(1)} fusion(f32[524288]{0:T(1024)S(1)} %bitcast.51, s32[1024]{0:T(1024)S(1)} %bitcast.61, f32[1024]{0:T(1024)S(1)} %bitcast.64), kind=kCustom, calls=%fused_computation.2 | custom fusion | flops 1024 | bytes 16384
  34.6 0.0 copy-start.9
  34.6 0.0 copy-start.5
  34.6 1.5 reshape.50
  36.2 1.1 fusion.43
  37.2 6.4 %collective-permute-start.6 = (f32[4,1,8,2048]{3,2,1,0:T(8,128)S(1)}, f32[4,1,8,2048]{3,2,1,0:T(8,128)S(1)}, u32[]{:S(2)}, u32[]{:S(2)}) collective-permute-start(f32[4,1,8,2048]{3,2,1,0:T(8,128)S(1)} %get-tuple-element.5), channel_id=1, source_target_pairs={{1,0},{2,1},{3,2},{4,3},{5,4},{6,5},{7,6},{8,7},{9,8},{10,9},{11,1... | collective-permute-start | bytes 786440 | tf_op jit(solution)/shard_map/ppermute | solution.py:17
  43.6 1.9 collective-permute-start.7
  45.6 0.0 collective-permute-done.2
  45.6 0.0 collective-permute-done.3
  45.6 1.5 collective-permute-done.6
  47.1 6.6 %collective-permute-done.7 = f32[4,1,8,2048]{3,2,1,0:T(8,128)S(1)} collective-permute-done((f32[4,1,8,2048]{3,2,1,0:T(8,128)S(1)}, f32[4,1,8,2048]{3,2,1,0:T(8,128)S(1)}, u32[]{:S(2)}, u32[]{:S(2)}) %collective-permute-start.7) | collective-permute-done | bytes 262176 | tf_op jit(solution)/shard_map/ppermute | solution.py:15
  53.7 15.9 %fusion.29 = (f32[4,8,8,2048]{3,2,1,0:T(8,128)}, f32[1,4,64,2048]{3,2,1,0:T(8,128)S(1)}) fusion(f32[4,8,8,2048]{3,2,1,0:T(8,128)} %reshape.50, f32[4,1,8,2048]{3,2,1,0:T(8,128)S(1)} %collective-permute-done.7, f32[4,1,8,2048]{3,2,1,0:T(8,128)S(1)} %collective-permute-done.6, f32[4,8,8,2048]{3,2,1,0:T(8,128)} %param.14, f32[8,8,2048]{2,1,0:T(8,128)S(1)} %copy-done.5, ...), kind=kLoop, calls=%fused_computation.49 | loop fusion | flops 13631488 | bytes 14155776 | tf_op jit(solution)/shard_map/add | solution.py:70
  69.7 1.4 copy.13
  71.0 0.7 scatter_fusion
  71.8 0.0 copy-start.8
  71.8 1.2 copy.22
  73.0 0.1 copy-done.1
  73.1 0.7 fusion.44
  73.8 1.9 collective-permute-start.4
  75.7 3.4 %collective-permute-start.5 = (f32[4,1,8,2048]{3,2,1,0:T(8,128)S(1)}, f32[4,1,8,2048]{3,2,1,0:T(8,128)S(1)}, u32[]{:S(2)}, u32[]{:S(2)}) collective-permute-start(f32[4,1,8,2048]{3,2,1,0:T(8,128)S(1)} %get-tuple-element.8), channel_id=1, source_target_pairs={{0,1},{1,2},{2,3},{3,4},{4,5},{5,6},{6,7},{7,8},{8,9},{9,10},{10,1... | collective-permute-start | bytes 786440 | tf_op jit(solution)/shard_map/ppermute | solution.py:15
  79.1 0.1 compare_reduce_fusion
  79.2 0.4 copy.17
  79.6 7.0 %scatter_fusion.3 = f32[524288]{0:T(1024)S(1)} fusion(f32[524288]{0:T(1024)S(1)} %bitcast.50, s32[1024]{0:T(1024)S(1)} %bitcast.62, f32[1024]{0:T(1024)S(1)} %bitcast.63), kind=kCustom, calls=%fused_computation.3 | custom fusion | flops 1024 | bytes 16384
  86.6 1.5 reshape.56
  88.1 0.0 collective-permute-done.4
  88.1 0.0 collective-permute-done.5
  88.1 8.4 %fusion.22 = f32[1,4,64,2048]{3,2,1,0:T(8,128)S(1)} fusion(f32[4,8,8,2048]{3,2,1,0:T(8,128)} %bitcast.56, f32[4,1,8,2048]{3,2,1,0:T(8,128)S(1)} %collective-permute-done.5, f32[4,1,8,2048]{3,2,1,0:T(8,128)S(1)} %collective-permute-done.4, f32[4,8,8,2048]{3,2,1,0:T(8,128)} %param.12, f32[8,8,2048]{2,1,0:T(8,128)S(1)} %copy-done.5), kind=kLoop, calls=%fused_computation.42 | loop fusion | flops 6815744 | bytes 7340032
  96.5 0.0 copy-start
  96.5 2.7 %copy.15 = f32[1,4,64,2048]{3,1,2,0:T(4,128)} copy(f32[1,4,64,2048]{3,2,1,0:T(8,128)S(1)} %fusion.22) | data formatting | bytes 4194304
  99.2 2.0 scatter_fusion.1
  101.2 7.8 %fusion.34 = f32[8,8,2048]{2,1,0:T(8,128)} fusion(f32[4,8,8,2048]{3,2,1,0:T(8,128)} %reshape.50, f32[4,8,8,2048]{3,2,1,0:T(8,128)S(1)} %copy-done, f32[1,4,64,2048]{3,1,2,0:T(4,128)} %bitcast.58, f32[4,8,8,2048]{3,2,1,0:T(8,128)} %reshape.56, f32[4,8,8,2048]{3,2,1,0:T(8,128)} %param.11, f32[4]{0:T(128)S(1)} %convert_element_type.12, ...), kind=kLoop, calls=%fused_computation.55 | loop fusion | flops 5636096 | bytes 13107216 | tf_op jit(solution)/shard_map/reduce_sum | solution.py:84
  109.1 0.0 all-reduce.6.cloned.1.call-update
  109.1 141.9 %all-reduce.6.cloned.1.call-done = f32[8,8,2048]{2,1,0:T(8,128)} async-done(((f32[8,8,2048]{2,1,0:T(8,128)}), f32[8,8,2048]{2,1,0:T(8,128)}) %all-reduce.6.cloned.1.call-update) | async-done | bytes 524304 | tf_op jit(solution)/shard_map/psum | solution.py:85
  251.0 1.9 broadcast_multiply_fusion
  (31 shorter events, 0.1 us)
Async XLA Ops:
  6.5 17.6 %copy-start.11 = (s32[2]{0:T(128)S(1)}, s32[2]{0:T(128)}, u32[]{:S(2)}) copy-start(s32[2]{0:T(128)} %constant.48) | copy-start | bytes 28
  6.5 17.7 %copy-start.10 = (s32[2]{0:T(128)S(1)}, s32[2]{0:T(128)}, u32[]{:S(2)}) copy-start(s32[2]{0:T(128)} %constant.45) | copy-start | bytes 28
  6.5 17.9 %copy-start.2 = (f32[4,8,8,2048]{3,2,1,0:T(8,128)S(1)}, f32[4,8,8,2048]{3,2,1,0:T(8,128)}, u32[]{:S(2)}) copy-start(f32[4,8,8,2048]{3,2,1,0:T(8,128)} %param.14) | copy-start | bytes 6291460
  6.5 17.5 %copy-start.12 = (s32[4]{0:T(128)S(1)}, s32[4]{0:T(128)}, u32[]{:S(2)}) copy-start(s32[4]{0:T(128)} %param.15) | copy-start | bytes 52
  6.5 17.6 %copy-start.7 = (s32[4,256]{1,0:T(4,128)S(1)}, s32[4,256]{1,0:T(4,128)}, u32[]{:S(2)}) copy-start(s32[4,256]{1,0:T(4,128)} %param.17) | copy-start | bytes 12292
  6.5 17.8 %copy-start.6 = (f32[4,2,256]{2,1,0:T(2,128)S(1)}, f32[4,2,256]{2,1,0:T(2,128)}, u32[]{:S(2)}) copy-start(f32[4,2,256]{2,1,0:T(2,128)} %param.18) | copy-start | bytes 24580
  6.6 244.4 %all-reduce.6.cloned.1.call-start = ((), (), s32[]{:S(2)}) async-start(), calls=%async_computation | async-start | bytes 1048576 | tf_op jit(solution)/shard_map/psum | solution.py:85
  8.6 15.8 %collective-permute-start = (f32[4,1,8,2048]{3,2,1,0:T(8,128)}, f32[4,1,8,2048]{3,2,1,0:T(8,128)S(1)}, u32[]{:S(2)}, u32[]{:S(2)}) collective-permute-start(f32[4,1,8,2048]{3,2,1,0:T(8,128)} %get-tuple-element.11), channel_id=1, source_target_pairs={{1,0},{2,1},{3,2},{4,3},{5,4},{6,5},{7,6},{8,7},{9,8},{10,9},{11,1... | collective-permute-start | bytes 786440 | tf_op jit(solution)/shard_map/ppermute | solution.py:17
  12.1 12.3 %collective-permute-start.1 = (f32[4,1,8,2048]{3,2,1,0:T(8,128)}, f32[4,1,8,2048]{3,2,1,0:T(8,128)S(1)}, u32[]{:S(2)}, u32[]{:S(2)}) collective-permute-start(f32[4,1,8,2048]{3,2,1,0:T(8,128)} %get-tuple-element.12), channel_id=1, source_target_pairs={{0,1},{1,2},{2,3},{3,4},{4,5},{5,6},{6,7},{7,8},{8,9},{9,10},{10,1... | collective-permute-start | bytes 786440 | tf_op jit(solution)/shard_map/ppermute | solution.py:15
  15.8 29.8 %collective-permute-start.2 = (f32[4,1,8,2048]{3,2,1,0:T(8,128)}, f32[4,1,8,2048]{3,2,1,0:T(8,128)S(1)}, u32[]{:S(2)}, u32[]{:S(2)}) collective-permute-start(f32[4,1,8,2048]{3,2,1,0:T(8,128)} %get-tuple-element.9), channel_id=1, source_target_pairs={{1,0},{2,1},{3,2},{4,3},{5,4},{6,5},{7,6},{8,7},{9,8},{10,9},{11,1... | collective-permute-start | bytes 786440 | tf_op jit(solution)/shard_map/ppermute | solution.py:17
  22.1 23.4 %collective-permute-start.3 = (f32[4,1,8,2048]{3,2,1,0:T(8,128)S(1)}, f32[4,1,8,2048]{3,2,1,0:T(8,128)S(1)}, u32[]{:S(2)}, u32[]{:S(2)}) collective-permute-start(f32[4,1,8,2048]{3,2,1,0:T(8,128)S(1)} %get-tuple-element.10), channel_id=1, source_target_pairs={{0,1},{1,2},{2,3},{3,4},{4,5},{5,6},{6,7},{7,8},{8,9},{9,10},{10,1... | collective-permute-start | bytes 786440 | tf_op jit(solution)/shard_map/ppermute | solution.py:15
  34.6 10.9 %copy-start.9 = (f32[4,2]{0,1:T(2,128)S(1)}, f32[4,2]{0,1:T(2,128)}, u32[]{:S(2)}) copy-start(f32[4,2]{0,1:T(2,128)} %param.16) | copy-start | bytes 100
  34.6 19.1 %copy-start.5 = (f32[8,8,2048]{2,1,0:T(8,128)S(1)}, f32[8,8,2048]{2,1,0:T(8,128)}, u32[]{:S(2)}) copy-start(f32[8,8,2048]{2,1,0:T(8,128)} %param.10) | copy-start | bytes 1572868
  37.2 9.9 %collective-permute-start.6 = (f32[4,1,8,2048]{3,2,1,0:T(8,128)S(1)}, f32[4,1,8,2048]{3,2,1,0:T(8,128)S(1)}, u32[]{:S(2)}, u32[]{:S(2)}) collective-permute-start(f32[4,1,8,2048]{3,2,1,0:T(8,128)S(1)} %get-tuple-element.5), channel_id=1, source_target_pairs={{1,0},{2,1},{3,2},{4,3},{5,4},{6,5},{7,6},{8,7},{9,8},{10,9},{11,1... | collective-permute-start | bytes 786440 | tf_op jit(solution)/shard_map/ppermute | solution.py:17
  43.6 10.1 %collective-permute-start.7 = (f32[4,1,8,2048]{3,2,1,0:T(8,128)S(1)}, f32[4,1,8,2048]{3,2,1,0:T(8,128)S(1)}, u32[]{:S(2)}, u32[]{:S(2)}) collective-permute-start(f32[4,1,8,2048]{3,2,1,0:T(8,128)S(1)} %get-tuple-element.6), channel_id=1, source_target_pairs={{0,1},{1,2},{2,3},{3,4},{4,5},{5,6},{6,7},{7,8},{8,9},{9,10},{10,1... | collective-permute-start | bytes 786440 | tf_op jit(solution)/shard_map/ppermute | solution.py:15
  71.7 1.3 copy-start.1
  71.8 7.3 %copy-start.8 = (s32[4,8]{1,0:T(4,128)S(1)}, s32[4,8]{1,0:T(4,128)}, u32[]{:S(2)}) copy-start(s32[4,8]{1,0:T(4,128)} %param.19) | copy-start | bytes 388
  71.8 7.4 %copy-start.4 = (f32[4,8,8,2048]{3,2,1,0:T(8,128)S(1)}, f32[4,8,8,2048]{3,2,1,0:T(8,128)}, u32[]{:S(2)}) copy-start(f32[4,8,8,2048]{3,2,1,0:T(8,128)} %get-tuple-element.13) | copy-start | bytes 6291460
  73.1 6.6 %copy-start.3 = (f32[1,4,64,2048]{3,2,1,0:T(8,128)}, f32[1,4,64,2048]{3,2,1,0:T(8,128)S(1)}, u32[]{:S(2)}) copy-start(f32[1,4,64,2048]{3,2,1,0:T(8,128)S(1)} %copy.22) | copy-start | bytes 6291460
  73.8 14.4 %collective-permute-start.4 = (f32[4,1,8,2048]{3,2,1,0:T(8,128)}, f32[4,1,8,2048]{3,2,1,0:T(8,128)S(1)}, u32[]{:S(2)}, u32[]{:S(2)}) collective-permute-start(f32[4,1,8,2048]{3,2,1,0:T(8,128)} %get-tuple-element.7), channel_id=1, source_target_pairs={{1,0},{2,1},{3,2},{4,3},{5,4},{6,5},{7,6},{8,7},{9,8},{10,9},{11,1... | collective-permute-start | bytes 786440 | tf_op jit(solution)/shard_map/ppermute | solution.py:17
  75.7 12.4 %collective-permute-start.5 = (f32[4,1,8,2048]{3,2,1,0:T(8,128)S(1)}, f32[4,1,8,2048]{3,2,1,0:T(8,128)S(1)}, u32[]{:S(2)}, u32[]{:S(2)}) collective-permute-start(f32[4,1,8,2048]{3,2,1,0:T(8,128)S(1)} %get-tuple-element.8), channel_id=1, source_target_pairs={{0,1},{1,2},{2,3},{3,4},{4,5},{5,6},{6,7},{7,8},{8,9},{9,10},{10,1... | collective-permute-start | bytes 786440 | tf_op jit(solution)/shard_map/ppermute | solution.py:15
  96.5 4.7 %copy-start = (f32[4,8,8,2048]{3,2,1,0:T(8,128)S(1)}, f32[4,8,8,2048]{3,2,1,0:T(8,128)}, u32[]{:S(2)}) copy-start(f32[4,8,8,2048]{3,2,1,0:T(8,128)} %param.12) | copy-start | bytes 6291460
Sparse Core Ops, SparseCore 0:
  109.2 141.7 all-reduce.5
where the time goes:
time: 262 us; the launch traced here: 260 us
  waiting for transfers between devices  150 us (57%)
  other arithmetic  53.9 us (21%)
  starting transfers between devices  27.3 us (10%)
  local copies, waits for them, and re-layouts  14.7 us (6%)
  between operations  13.8 us (5%)
    psum x1, waiting for transfers between devices, body(): total = lax.psum(partial_image, 'shot')  142 us
    unnamed x6, other arithmetic  22.4 us
    add x2, other arithmetic, advance(): 2.0 * now - before + velocity_term * laplace(padded)  18.9 us
    ppermute x4, starting transfers between devices, extended(): lax.ppermute(head, axis, [((i + 1) % count, i) for i in range(ends)])  18.1 us
    ppermute x4, starting transfers between devices, extended(): lax.ppermute(tail, axis, [(i, (i + 1) % count) for i in range(ends)])  9.12 us
    reduce_sum x1, other arithmetic, body(): partial_image = jnp.sum(image * inside[:, None, None, None], axis=0)  7.84 us
    ppermute x4, waiting for transfers between devices, extended(): lax.ppermute(tail, axis, [(i, (i + 1) % count) for i in range(ends)])  6.61 us
    unnamed x32, local copies, waits for them, and re-layouts  6.14 us
  transfers between devices with their start and end apart: 9, of which 3 were waited for; matrix products, arithmetic and copies ran while one was open for 9% of the time, Pallas kernels for 0%

commit v1 on v0

v1 whole, which is shorter than its diff:
```python
import functools

import jax
import jax.numpy as jnp
from jax import lax
from jax.experimental import pallas as pl
from jax.experimental.pallas import tpu as pltpu
from jax.sharding import PartitionSpec as P

MESH = pl.DeviceIdType.MESH
SHOTS = 4
PLANES = 8
LEVELS = 8
COLUMNS = 2048
LANES = 128
TILES = COLUMNS // LANES
RECEIVERS = 256
GROUP = 16
HALF = COLUMNS // 2
CELLS = PLANES * LEVELS * COLUMNS
EIGHTH = COLUMNS // 8
UP, DOWN = 0, 1
ENDS = (PLANES, 1)
GHOSTS = (0, PLANES + 1)


def kernel(
    scale,
    vel_hbm,
    wave_prev_hbm,
    wave_now_hbm,
    adj_next_hbm,
    adj_now_hbm,
    source_cell,
    source_wave,
    cells_ref,
    residual_ref,
    aperture,
    out_ref,
    vel,
    wave0,
    wave1,
    adj0,
    adj1,
    prev,
    after,
    injected,
    inner,
    edge,
    edge_out,
    relay_buf,
    inner_got,
    inner_part,
    pair_got,
    edge_got,
    load_sem,
    vel_sem,
    send_sem,
    recv_sem,
    relay_send,
    relay_recv,
    red_send,
    red_recv,
    pair_sem,
    gather_send,
    gather_recv,
    edge_send,
    edge_recv,
    spread_send,
    spread_recv,
):
    shot = lax.axis_index("shot")
    dom = lax.axis_index("dom")
    column = lax.rem(dom, 4)
    row = dom // 4
    lower = lax.rem(shot // 2, 2)
    eighth = (shot // 4) * 2 + lax.rem(shot, 2)

    def along_dom(step):
        return {"dom": lax.rem(dom + step + GROUP, GROUP)}

    def member(index):
        return {"shot": (index // 2) * 4 + lower * 2 + lax.rem(index, 2)}

    towards = (along_dom(1), along_dom(-1))
    has = (dom < GROUP - 1, dom > 0)
    from_has = (dom > 0, dom < GROUP - 1)
    crosses = (column == 3, column == 0)
    from_crosses = (column == 0, column == 3)
    relays = ((column == 0) & (row < 3), (column == 3) & (row > 0))
    relay_first = (along_dom(-3), along_dom(3))
    relay_second = (along_dom(4), along_dom(-4))

    def load(s):
        return [
            pltpu.make_async_copy(source.at[s], target, load_sem.at[s, k])
            for k, (source, target) in enumerate(
                (
                    (wave_now_hbm, wave0.at[s, pl.ds(1, PLANES)]),
                    (adj_now_hbm, adj0.at[s, pl.ds(1, PLANES)]),
                    (wave_prev_hbm, prev.at[s]),
                    (adj_next_hbm, after.at[s]),
                )
            )
        ]

    vel_load = pltpu.make_async_copy(vel_hbm, vel, vel_sem)
    vel_load.start()
    for s in range(SHOTS):
        for copy in load(s):
            copy.start()

    barrier = pltpu.get_barrier_semaphore()

    def greet(device):
        pl.semaphore_signal(barrier, inc=1, device_id=device, device_id_type=MESH)

    def greet_peer(k, carry):
        greet({"shot": lax.rem(shot + k, GROUP)})
        return carry

    lax.fori_loop(1, GROUP, greet_peer, 0)
    greet(towards[UP])
    greet(towards[DOWN])

    @pl.when(column == 0)
    def _():
        greet(along_dom(3))
        greet(along_dom(4))
        greet(along_dom(-4))

    @pl.when(column == 3)
    def _():
        greet(along_dom(-3))
        greet(along_dom(4))
        greet(along_dom(-4))

    relaying = (column == 0) | (column == 3)
    pl.semaphore_wait(barrier, GROUP + 1 + jnp.where(relaying, 3, 0))

    blocks = ((wave0, adj0), (wave1, adj1))

    def layer_refs(step, field, s, way):
        block = blocks[step][field]
        if step == 0:
            source = (wave_now_hbm, adj_now_hbm)[field].at[s, ENDS[way] - 1]
        else:
            source = block.at[s, ENDS[way]]
        return source, block.at[s, GHOSTS[way]]

    def remote(source, target, send, recv, device):
        return pltpu.make_async_remote_copy(
            src_ref=source,
            dst_ref=target,
            send_sem=send,
            recv_sem=recv,
            device_id=device,
            device_id_type=MESH,
        )

    first_half, second_half = pl.ds(0, HALF), pl.ds(HALF, HALF)

    def whole(step, field, s, way):
        source, target = layer_refs(step, field, s, way)
        k = 2 * step + field
        return remote(source, target, send_sem.at[way, k, s], recv_sem.at[way, k, s], towards[way])

    def direct(step, field, s, way):
        source, target = layer_refs(step, field, s, way)
        k = 2 * step + field
        return remote(
            source.at[:, first_half],
            target.at[:, first_half],
            send_sem.at[way, k, s],
            recv_sem.at[way, k, s],
            towards[way],
        )

    def leg_one(step, field, s, way):
        source, _ = layer_refs(step, field, s, way)
        k = 2 * step + field
        return remote(
            source.at[:, second_half],
            relay_buf.at[k, s],
            relay_send.at[0, k, s],
            relay_recv.at[0, k, s],
            relay_first[way],
        )

    def leg_two(step, field, s, way):
        _, target = layer_refs(step, field, s, way)
        k = 2 * step + field
        return remote(
            relay_buf.at[k, s],
            target.at[:, second_half],
            relay_send.at[1, k, s],
            relay_recv.at[1, k, s],
            relay_second[way],
        )

    def send_layers(step, s):
        for field in (0, 1):
            for way in (UP, DOWN):

                @pl.when(has[way] & crosses[way])
                def _():
                    leg_one(step, field, s, way).start()
                    direct(step, field, s, way).start()

                @pl.when(has[way] & jnp.logical_not(crosses[way]))
                def _():
                    whole(step, field, s, way).start()

    def pass_on(step, s):
        for field in (0, 1):
            for way in (UP, DOWN):

                @pl.when(relays[way])
                def _():
                    leg_one(step, field, s, way).wait_recv()
                    leg_two(step, field, s, way).start()

    def take_layers(step, s):
        for field in (0, 1):
            for way in (UP, DOWN):

                @pl.when(from_has[way] & from_crosses[way])
                def _():
                    direct(step, field, s, way).wait_recv()
                    leg_two(step, field, s, way).wait_recv()

                @pl.when(from_has[way] & jnp.logical_not(from_crosses[way]))
                def _():
                    whole(step, field, s, way).wait_recv()

    def end_sends(step, s):
        for field in (0, 1):
            for way in (UP, DOWN):

                @pl.when(has[way] & crosses[way])
                def _():
                    leg_one(step, field, s, way).wait_send()
                    direct(step, field, s, way).wait_send()

                @pl.when(has[way] & jnp.logical_not(crosses[way]))
                def _():
                    whole(step, field, s, way).wait_send()

                @pl.when(relays[way])
                def _():
                    leg_two(step, field, s, way).wait_send()

    def each_shot(body):
        def step(s, carry):
            body(s)
            return carry

        lax.fori_loop(0, SHOTS, step, 0)

    each_shot(lambda s: send_layers(0, s))

    for way in (UP, DOWN):

        @pl.when(jnp.logical_not(from_has[way]))
        def _():
            def clear(s):
                nothing = jnp.zeros((LEVELS, COLUMNS), jnp.float32)
                for block in (wave0, adj0, wave1, adj1):
                    block[s, GHOSTS[way]] = nothing

            each_shot(clear)

    level = lax.broadcasted_iota(jnp.int32, (LEVELS, LANES), 0)
    lane = lax.broadcasted_iota(jnp.int32, (LEVELS, LANES), 1)
    place = level * LANES + lane
    top, bottom = level == 0, level == LEVELS - 1
    leftmost, rightmost = lane == 0, lane == LANES - 1

    def columns_of(t):
        return pl.ds(t * LANES, LANES)

    def laplace(ref, s, x):
        empty = jnp.zeros((LEVELS, LANES), jnp.float32)
        here = ref[s, x, :, columns_of(0)]
        right_of = pltpu.roll(here, LANES - 1, 1)
        before = empty
        for t in range(TILES):
            if t + 1 < TILES:
                following = ref[s, x, :, columns_of(t + 1)]
                right_next = pltpu.roll(following, LANES - 1, 1)
            else:
                following, right_next = empty, empty
            shifted = pltpu.roll(here, 1, 1)
            left = jnp.where(leftmost, before, shifted)
            right = jnp.where(rightmost, right_next, right_of)
            above = jnp.where(top, 0.0, pltpu.roll(here, 1, 0))
            below = jnp.where(bottom, 0.0, pltpu.roll(here, LEVELS - 1, 0))
            beside = ref[s, x - 1, :, columns_of(t)] + ref[s, x + 1, :, columns_of(t)]
            beside = (beside + (above + below)) + (left + right)
            yield here, beside - 6.0 * here
            before, here, right_of = shifted, following, right_next

    def source_of(s):
        local = source_cell[s] - dom * CELLS
        tile = (local >> 14) * TILES + ((local >> 7) & (TILES - 1))
        return (tile * LEVELS + ((local >> 11) & (LEVELS - 1))) * LANES + (local & (LANES - 1))

    def rows_of(x, t):
        return pl.ds(pl.multiple_of(((x - 1) * TILES + t) * LEVELS, LEVELS), LEVELS)

    def first_step(s, x):
        at = source_of(s) - (x - 1) * (TILES * LEVELS * LANES)
        wavelet = source_wave[s, 0]
        both = zip(laplace(wave0, s, x), laplace(adj0, s, x), strict=True)
        for t, ((wave, wave_lap), (adj, adj_lap)) in enumerate(both):
            cols = columns_of(t)
            v = vel[x - 1, :, cols]
            pushed = v * wave_lap + jnp.where(place == at - t * (LEVELS * LANES), wavelet, 0.0)
            wave1[s, x, :, cols] = (2.0 * wave - prev[s, x - 1, :, cols]) + pushed
            prev[s, x - 1, :, cols] = pushed
            drawn = injected[s, rows_of(x, t), pl.ds(0, LANES)]
            adj1[s, x, :, cols] = (2.0 * adj - after[s, x - 1, :, cols]) + (v * adj_lap + drawn)

    def second_step(s, x, total, place_x, first):
        at = source_of(s) - (x - 1) * (TILES * LEVELS * LANES)
        wavelet = source_wave[s, 1]
        inside = aperture[s, 0] == dom
        for k in range(1, 8):
            inside = inside | (aperture[s, k] == dom)
        weight = jnp.where(inside, scale, 0.0)
        both = zip(laplace(wave1, s, x), laplace(adj1, s, x), strict=True)
        for t, ((_, wave_lap), (adj, adj_lap)) in enumerate(both):
            cols = columns_of(t)
            v = vel[x - 1, :, cols]
            pushed = v * wave_lap + jnp.where(place == at - t * (LEVELS * LANES), wavelet, 0.0)
            drawn = injected[s, rows_of(x, t), pl.ds(LANES, LANES)]
            zero = (2.0 * adj - adj0[s, x, :, cols]) + (v * adj_lap + drawn)
            image = weight * (adj * pushed + zero * prev[s, x - 1, :, cols])
            total[place_x, :, cols] = image if first else total[place_x, :, cols] + image

    def inject(s):
        local = cells_ref[pl.ds(s, 1), :] - dom * CELLS
        tile = (local >> 14) * TILES + ((local >> 7) & (TILES - 1))
        line = tile * LEVELS + ((local >> 11) & (LEVELS - 1))
        spot = local & (LANES - 1)
        lines = PLANES * TILES * LEVELS
        picks = lax.broadcasted_iota(jnp.int32, (lines, RECEIVERS), 0) == line
        picks = jnp.where(picks, 1.0, 0.0).astype(jnp.bfloat16)
        hits = lax.broadcasted_iota(jnp.int32, (LANES, RECEIVERS), 0) == spot
        parts = []
        for step in (0, 1):
            rest = residual_ref[s, pl.ds(step, 1), :]
            pieces = []
            for _ in range(3):
                piece = rest.astype(jnp.bfloat16).astype(jnp.float32)
                rest = rest - piece
                pieces.append(jnp.where(hits, piece, 0.0).astype(jnp.bfloat16))
            parts.append(jnp.concatenate(pieces, axis=1))
        injected[s] = lax.dot_general(
            jnp.concatenate([picks] * 3, axis=1),
            jnp.concatenate(parts, axis=0),
            (((1,), (1,)), ((), ())),
            preferred_element_type=jnp.float32,
        )

    def planes(first, last, body):
        def step(x, carry):
            body(x)
            return carry

        lax.fori_loop(first, last, step, 0)

    vel_load.wait()

    def inner_first(s):
        inject(s)
        for copy in load(s):
            copy.wait()
        planes(2, PLANES, lambda x: first_step(s, x))

    each_shot(inner_first)

    def clear_inner(x):
        inner[x] = jnp.zeros((LEVELS, COLUMNS), jnp.float32)

    planes(0, PLANES - 2, clear_inner)

    def ends_first(s):
        pass_on(0, s)
        take_layers(0, s)
        planes(0, 2, lambda k: first_step(s, 1 + k * (PLANES - 1)))
        send_layers(1, s)
        planes(2, PLANES, lambda x: second_step(s, x, inner, x - 2, False))

    each_shot(ends_first)

    def eighth_of(index):
        return pl.ds(pl.multiple_of(index * EIGHTH, EIGHTH), EIGHTH)

    def scatter(k):
        peer = lax.rem(eighth + k, 8)
        return remote(
            inner.at[:, :, eighth_of(peer)],
            inner_got.at[k],
            red_send.at[k],
            red_recv.at[k],
            member(peer),
        )

    def gather(k):
        mine = out_ref.at[pl.ds(1, PLANES - 2), :, eighth_of(eighth)]
        return remote(
            mine, mine, gather_send.at[k], gather_recv.at[k], member(lax.rem(eighth + k, 8))
        )

    def gathered(k):
        peer = lax.rem(eighth - k + 8, 8)
        there = out_ref.at[pl.ds(1, PLANES - 2), :, eighth_of(peer)]
        return remote(there, there, gather_send.at[k], gather_recv.at[k], member(peer))

    def every(count, body):
        def step(k, carry):
            body(k)
            return carry

        lax.fori_loop(1, count, step, 0)

    every(8, lambda k: scatter(k).start())

    def clear_edge(x):
        edge[x] = jnp.zeros((LEVELS, COLUMNS), jnp.float32)

    planes(0, 2, clear_edge)

    def ends_second(s):
        pass_on(1, s)
        take_layers(1, s)
        planes(0, 2, lambda k: second_step(s, 1 + k * (PLANES - 1), edge, k, False))

    ends_second(0)

    inner_part[...] = inner[:, :, eighth_of(eighth)]

    def add_inner(k):
        scatter(k).wait_recv()
        inner_part[...] += inner_got[k]

    every(8, add_inner)
    swap = remote(
        inner_part,
        pair_got,
        pair_sem.at[0],
        pair_sem.at[1],
        {"shot": shot + 2 - 4 * lower},
    )
    swap.start()

    ends_second(1)

    swap.wait_recv()
    out_ref[pl.ds(1, PLANES - 2), :, eighth_of(eighth)] = inner_part[...] + pair_got[...]
    every(8, lambda k: gather(k).start())

    ends_second(2)
    ends_second(3)

    def lane_tile(index):
        return pl.ds(pl.multiple_of(index * LANES, LANES), LANES)

    def scatter_edge(k):
        peer = lax.rem(shot + k, GROUP)
        return remote(
            edge.at[:, :, lane_tile(peer)],
            edge_got.at[k],
            edge_send.at[k],
            edge_recv.at[k],
            {"shot": peer},
        )

    def spread(k):
        mine = edge_out.at[:, :, lane_tile(shot)]
        return remote(
            mine, mine, spread_send.at[k], spread_recv.at[k], {"shot": lax.rem(shot + k, GROUP)}
        )

    def spread_from(k):
        peer = lax.rem(shot - k + GROUP, GROUP)
        there = edge_out.at[:, :, lane_tile(peer)]
        return remote(there, there, spread_send.at[k], spread_recv.at[k], {"shot": peer})

    every(GROUP, lambda k: scatter_edge(k).start())

    def add_edge(k, carry):
        scatter_edge(k).wait_recv()
        return carry + edge_got[k]

    edge_out[:, :, lane_tile(shot)] = lax.fori_loop(1, GROUP, add_edge, edge[:, :, lane_tile(shot)])
    every(GROUP, lambda k: spread(k).start())

    for step in (0, 1):
        each_shot(functools.partial(end_sends, step))
    swap.wait_send()
    every(8, lambda k: scatter(k).wait_send())
    every(8, lambda k: gather(k).wait_send())
    every(8, lambda k: gathered(k).wait_recv())
    every(GROUP, lambda k: scatter_edge(k).wait_send())
    every(GROUP, lambda k: spread(k).wait_send())
    every(GROUP, lambda k: spread_from(k).wait_recv())
    out_ref[0] = edge_out[0]
    out_ref[PLANES - 1] = edge_out[1]


def body(*arguments):
    scale = float(lax.axis_size("shot") * SHOTS) ** (-0.5)
    f32 = jnp.float32
    block = (LEVELS, COLUMNS)
    dma = pltpu.SemaphoreType.DMA
    hbm = pl.BlockSpec(memory_space=pltpu.HBM)
    vmem = pl.BlockSpec(memory_space=pltpu.VMEM)
    smem = pl.BlockSpec(memory_space=pltpu.SMEM)
    return pl.pallas_call(
        functools.partial(kernel, scale),
        out_shape=jax.ShapeDtypeStruct((PLANES, *block), f32),
        in_specs=[hbm, hbm, hbm, hbm, hbm, smem, smem, vmem, vmem, smem],
        out_specs=vmem,
        scratch_shapes=[
            pltpu.VMEM((PLANES, *block), f32),
            pltpu.VMEM((SHOTS, PLANES + 2, *block), f32),
            pltpu.VMEM((SHOTS, PLANES + 2, *block), f32),
            pltpu.VMEM((SHOTS, PLANES + 2, *block), f32),
            pltpu.VMEM((SHOTS, PLANES + 2, *block), f32),
            pltpu.VMEM((SHOTS, PLANES, *block), f32),
            pltpu.VMEM((SHOTS, PLANES, *block), f32),
            pltpu.VMEM((SHOTS, CELLS // LANES, 2 * LANES), f32),
            pltpu.VMEM((PLANES - 2, *block), f32),
            pltpu.VMEM((2, *block), f32),
            pltpu.VMEM((2, *block), f32),
            pltpu.VMEM((4, SHOTS, LEVELS, HALF), f32),
            pltpu.VMEM((8, PLANES - 2, LEVELS, EIGHTH), f32),
            pltpu.VMEM((PLANES - 2, LEVELS, EIGHTH), f32),
            pltpu.VMEM((PLANES - 2, LEVELS, EIGHTH), f32),
            pltpu.VMEM((GROUP, 2, LEVELS, LANES), f32),
            dma((SHOTS, 4)),
            dma,
            dma((2, 4, SHOTS)),
            dma((2, 4, SHOTS)),
            dma((2, 4, SHOTS)),
            dma((2, 4, SHOTS)),
            dma((8,)),
            dma((8,)),
            dma((2,)),
            dma((8,)),
            dma((8,)),
            dma((GROUP,)),
            dma((GROUP,)),
            dma((GROUP,)),
            dma((GROUP,)),
        ],
        compiler_params=pltpu.CompilerParams(
            collective_id=0, has_side_effects=True, vmem_limit_bytes=48 * 2**20
        ),
        name="gradient",
    )(*arguments)


def solution(mesh):
    placed = (
        P("dom", None, None),
        P("shot", "dom", None, None),
        P("shot", "dom", None, None),
        P("shot", "dom", None, None),
        P("shot", "dom", None, None),
        P("shot"),
        P("shot", None),
        P("shot", None),
        P("shot", None, None),
        P("shot", None),
    )
    return jax.shard_map(
        body, mesh=mesh, in_specs=placed, out_specs=P("dom", None, None), check_vma=False
    )
```

time: 262 us -> 74.5 us (0.28)
  the two profiles are of different devices: /device:TPU:65 before, /device:TPU:7 now
where the time goes in v1:
time: 74.5 us; the launch traced here: 74.2 us
  Pallas kernels  65.7 us (88%)
  local copies, waits for them, and re-layouts  8.5 us (11%)
    pallas_call x1, Pallas kernels, body(): pl.pallas_call(functools.partial(kernel, scale), out_shape=jax.ShapeDtype...  65.7 us
    unnamed x16, local copies, waits for them, and re-layouts  8.5 us

profile of v1, /device:TPU:7, one launch (start us, length us, event | category | flops | bytes accessed | tf_op | source)
XLA Modules:
  0.0 74.2 jit_solution(9575084909840112525)
XLA Ops:
  0.0 0.8 %copy.11.source_wave = f32[4,2]{1,0:T(4,128)S(1)} copy(f32[4,2]{0,1:T(2,128)} %param.16) | data formatting | bytes 64 | tf_op args[6]
  0.8 0.0 copy-start
  0.8 1.6 %copy-done = f32[4,8,8,2048]{3,2,1,0:T(8,128)S(1)} copy-done((f32[4,8,8,2048]{3,2,1,0:T(8,128)S(1)}, f32[4,8,8,2048]{3,2,1,0:T(8,128)}, u32[]{:S(2)}) %copy-start) | copy-done | bytes 2097176
  2.4 0.0 copy-start.1
  2.4 1.6 %copy-done.1 = f32[4,8,8,2048]{3,2,1,0:T(8,128)S(1)} copy-done((f32[4,8,8,2048]{3,2,1,0:T(8,128)S(1)}, f32[4,8,8,2048]{3,2,1,0:T(8,128)}, u32[]{:S(2)}) %copy-start.1) | copy-done | bytes 2097176
  3.9 0.0 copy-start.2
  4.0 1.0 %copy-done.2 = f32[8,8,2048]{2,1,0:T(8,128)S(1)} copy-done((f32[8,8,2048]{2,1,0:T(8,128)S(1)}, f32[8,8,2048]{2,1,0:T(8,128)}, u32[]{:S(2)}) %copy-start.2) | copy-done | bytes 524312
  5.0 0.0 copy-start.3
  5.0 0.7 copy-done.3
  5.7 0.0 copy-start.4
  5.7 0.7 copy-done.4
  6.4 0.0 copy-start.5
  6.4 0.7 copy-done.5
  7.1 0.0 copy-start.6
  7.1 0.7 copy-done.6
  7.7 65.7 %gradient.1 = f32[8,8,2048]{2,1,0:T(8,128)S(1)} custom-call(f32[8,8,2048]{2,1,0:T(8,128)S(1)} %copy-done.2, f32[4,8,8,2048]{3,2,1,0:T(8,128)S(1)} %copy-done, f32[4,8,8,2048]{3,2,1,0:T(8,128)S(1)} %copy-done.1, f32[4,8,8,2048]{3,2,1,0:T(8,128)} %adj_next_hbm.1, f32[4,8,8,2048]{3,2,1,0:T(8,128)} %adj_now_hbm.1, s32[4]{0:T(128)S(1)} %copy-done.6, ...), custom_call_target="tpu_custom_call" | custom-call | tf_op jit(solution)/shard_map/gradient/pallas_call | solution.py:521
  73.4 0.8 %copy.13 = f32[8,8,2048]{2,1,0:T(8,128)} copy(f32[8,8,2048]{2,1,0:T(8,128)S(1)} %gradient.1) | data formatting | bytes 1048576
Async XLA Ops:
  0.8 1.6 %copy-start = (f32[4,8,8,2048]{3,2,1,0:T(8,128)S(1)}, f32[4,8,8,2048]{3,2,1,0:T(8,128)}, u32[]{:S(2)}) copy-start(f32[4,8,8,2048]{3,2,1,0:T(8,128)} %wave_prev_hbm.1) | copy-start | bytes 6291460
  2.4 1.6 %copy-start.1 = (f32[4,8,8,2048]{3,2,1,0:T(8,128)S(1)}, f32[4,8,8,2048]{3,2,1,0:T(8,128)}, u32[]{:S(2)}) copy-start(f32[4,8,8,2048]{3,2,1,0:T(8,128)} %wave_now_hbm.1) | copy-start | bytes 6291460
  3.9 1.0 %copy-start.2 = (f32[8,8,2048]{2,1,0:T(8,128)S(1)}, f32[8,8,2048]{2,1,0:T(8,128)}, u32[]{:S(2)}) copy-start(f32[8,8,2048]{2,1,0:T(8,128)} %vel_hbm.1) | copy-start | bytes 1572868
  5.0 0.7 copy-start.3
  5.7 0.7 copy-start.4
  6.4 0.7 copy-start.5
  7.1 0.7 copy-start.6

commit v2 on v1

--- a/solution.py
+++ b/solution.py
@@ -31,12 +31,17 @@
     wave_now_hbm,
     adj_next_hbm,
     adj_now_hbm,
+    source_cell_hbm,
+    source_wave_hbm,
+    cells_hbm,
+    residual_hbm,
+    aperture_hbm,
+    out_ref,
     source_cell,
     source_wave,
     cells_ref,
     residual_ref,
     aperture,
-    out_ref,
     vel,
     wave0,
     wave1,
@@ -48,13 +53,17 @@
     inner,
     edge,
     edge_out,
+    ends,
+    vel_ghost,
     relay_buf,
     inner_got,
     inner_part,
     pair_got,
     edge_got,
     load_sem,
-    vel_sem,
+    small_sem,
+    vel_send,
+    vel_recv,
     send_sem,
     recv_sem,
     relay_send,
@@ -104,8 +113,21 @@
             )
         ]
 
-    vel_load = pltpu.make_async_copy(vel_hbm, vel, vel_sem)
-    vel_load.start()
+    small_loads = [
+        pltpu.make_async_copy(source, target, small_sem.at[k])
+        for k, (source, target) in enumerate(
+            (
+                (cells_hbm, cells_ref),
+                (residual_hbm, residual_ref),
+                (vel_hbm, vel),
+                (source_cell_hbm, source_cell),
+                (source_wave_hbm, source_wave),
+                (aperture_hbm, aperture),
+            )
+        )
+    ]
+    for copy in small_loads:
+        copy.start()
     for s in range(SHOTS):
         for copy in load(s):
             copy.start()
@@ -138,14 +160,11 @@
     relaying = (column == 0) | (column == 3)
     pl.semaphore_wait(barrier, GROUP + 1 + jnp.where(relaying, 3, 0))
 
-    blocks = ((wave0, adj0), (wave1, adj1))
-
-    def layer_refs(step, field, s, way):
-        block = blocks[step][field]
-        if step == 0:
-            source = (wave_now_hbm, adj_now_hbm)[field].at[s, ENDS[way] - 1]
-        else:
-            source = block.at[s, ENDS[way]]
+    fields = ((wave_now_hbm, wave0), (adj_now_hbm, adj0), (None, wave1), (None, adj1))
+
+    def layer_refs(k, s, way):
+        given, block = fields[k]
+        source = ends.at[way, k - 2, s] if given is None else given.at[s, ENDS[way] - 1]
         return source, block.at[s, GHOSTS[way]]
 
     def remote(source, target, send, recv, device):
@@ -160,14 +179,12 @@
 
     first_half, second_half = pl.ds(0, HALF), pl.ds(HALF, HALF)
 
-    def whole(step, field, s, way):
-        source, target = layer_refs(step, field, s, way)
-        k = 2 * step + field
+    def whole(k, s, way):
+        source, target = layer_refs(k, s, way)
         return remote(source, target, send_sem.at[way, k, s], recv_sem.at[way, k, s], towards[way])
 
-    def direct(step, field, s, way):
-        source, target = layer_refs(step, field, s, way)
-        k = 2 * step + field
+    def direct(k, s, way):
+        source, target = layer_refs(k, s, way)
         return remote(
             source.at[:, first_half],
             target.at[:, first_half],
@@ -176,9 +193,8 @@
             towards[way],
         )
 
-    def leg_one(step, field, s, way):
-        source, _ = layer_refs(step, field, s, way)
-        k = 2 * step + field
+    def leg_one(k, s, way):
+        source, _ = layer_refs(k, s, way)
         return remote(
             source.at[:, second_half],
             relay_buf.at[k, s],
@@ -187,9 +203,8 @@
             relay_first[way],
         )
 
-    def leg_two(step, field, s, way):
-        _, target = layer_refs(step, field, s, way)
-        k = 2 * step + field
+    def leg_two(k, s, way):
+        _, target = layer_refs(k, s, way)
         return remote(
             relay_buf.at[k, s],
             target.at[:, second_half],
@@ -198,57 +213,59 @@
             relay_second[way],
         )
 
-    def send_layers(step, s):
-        for field in (0, 1):
-            for way in (UP, DOWN):
-
-                @pl.when(has[way] & crosses[way])
-                def _():
-                    leg_one(step, field, s, way).start()
-                    direct(step, field, s, way).start()
-
-                @pl.when(has[way] & jnp.logical_not(crosses[way]))
-                def _():
-                    whole(step, field, s, way).start()
-
-    def pass_on(step, s):
-        for field in (0, 1):
-            for way in (UP, DOWN):
-
-                @pl.when(relays[way])
-                def _():
-                    leg_one(step, field, s, way).wait_recv()
-                    leg_two(step, field, s, way).start()
-
-    def take_layers(step, s):
-        for field in (0, 1):
-            for way in (UP, DOWN):
-
-                @pl.when(from_has[way] & from_crosses[way])
-                def _():
-                    direct(step, field, s, way).wait_recv()
-                    leg_two(step, field, s, way).wait_recv()
-
-                @pl.when(from_has[way] & jnp.logical_not(from_crosses[way]))
-                def _():
-                    whole(step, field, s, way).wait_recv()
-
-    def end_sends(step, s):
-        for field in (0, 1):
-            for way in (UP, DOWN):
-
-                @pl.when(has[way] & crosses[way])
-                def _():
-                    leg_one(step, field, s, way).wait_send()
-                    direct(step, field, s, way).wait_send()
-
-                @pl.when(has[way] & jnp.logical_not(crosses[way]))
-                def _():
-                    whole(step, field, s, way).wait_send()
-
-                @pl.when(relays[way])
-                def _():
-                    leg_two(step, field, s, way).wait_send()
+    def when_each(conditions, body):
+        for way in (UP, DOWN):
+            pl.when(conditions[way])(functools.partial(body, way))
+
+    def both(one, other):
+        return tuple(a & b for a, b in zip(one, other, strict=True))
+
+    def but(one, other):
+        return tuple(a & jnp.logical_not(b) for a, b in zip(one, other, strict=True))
+
+    far, near = both(has, crosses), but(has, crosses)
+    from_far, from_near = both(from_has, from_crosses), but(from_has, from_crosses)
+
+    def send_first_legs(k, s):
+        when_each(far, lambda way: leg_one(k, s, way).start())
+
+    def send_layer(k, s):
+        when_each(far, lambda way: direct(k, s, way).start())
+        when_each(near, lambda way: whole(k, s, way).start())
+
+    def advance(k, s):
+        when_each(far, lambda way: direct(k, s, way).wait_send())
+        when_each(near, lambda way: whole(k, s, way).wait_send())
+        pl.when(s < SHOTS - 2)(lambda: send_layer(k, s + 2))
+        if k < 3:
+            pl.when(s >= SHOTS - 2)(lambda: send_layer(k + 1, s + 2 - SHOTS))
+
+        def pass_on(way):
+            leg_one(k, s, way).wait_recv()
+            leg_two(k, s, way).start()
+
+        when_each(relays, pass_on)
+
+    def take_layer(k, s):
+        def two_halves(way):
+            direct(k, s, way).wait_recv()
+            leg_two(k, s, way).wait_recv()
+
+        when_each(from_far, two_halves)
+        when_each(from_near, lambda way: whole(k, s, way).wait_recv())
+
+    def end_legs(k, s):
+        when_each(far, lambda way: leg_one(k, s, way).wait_send())
+        when_each(relays, lambda way: leg_two(k, s, way).wait_send())
+
+    def vel_layer(way):
+        return remote(
+            vel_hbm.at[ENDS[way] - 1],
+            vel_ghost.at[way],
+            vel_send.at[way],
+            vel_recv.at[way],
+            towards[way],
+        )
 
     def each_shot(body):
         def step(s, carry):
@@ -257,18 +274,23 @@
 
         lax.fori_loop(0, SHOTS, step, 0)
 
-    each_shot(lambda s: send_layers(0, s))
-
-    for way in (UP, DOWN):
-
-        @pl.when(jnp.logical_not(from_has[way]))
-        def _():
-            def clear(s):
-                nothing = jnp.zeros((LEVELS, COLUMNS), jnp.float32)
-                for block in (wave0, adj0, wave1, adj1):
-                    block[s, GHOSTS[way]] = nothing
-
-            each_shot(clear)
+    for k in (0, 1):
+        each_shot(functools.partial(send_first_legs, k))
+    when_each(has, lambda way: vel_layer(way).start())
+    send_layer(0, 0)
+    send_layer(0, 1)
+
+    def clear_ghosts(way):
+        nothing = jnp.zeros((LEVELS, COLUMNS), jnp.float32)
+        vel_ghost[way] = nothing
+
+        def clear(s):
+            for block in (wave0, adj0, wave1, adj1):
+                block[s, GHOSTS[way]] = nothing
+
+        each_shot(clear)
+
+    when_each(tuple(jnp.logical_not(there) for there in from_has), clear_ghosts)
 
     level = lax.broadcasted_iota(jnp.int32, (LEVELS, LANES), 0)
     lane = lax.broadcasted_iota(jnp.int32, (LEVELS, LANES), 1)
@@ -279,7 +301,8 @@
     def columns_of(t):
         return pl.ds(t * LANES, LANES)
 
-    def laplace(ref, s, x):
+    def laplace(ref, s, x, sides=None):
+        sides = (x - 1, x + 1) if sides is None else sides
         empty = jnp.zeros((LEVELS, LANES), jnp.float32)
         here = ref[s, x, :, columns_of(0)]
         right_of = pltpu.roll(here, LANES - 1, 1)
@@ -295,8 +318,9 @@
             right = jnp.where(rightmost, right_next, right_of)
             above = jnp.where(top, 0.0, pltpu.roll(here, 1, 0))
             below = jnp.where(bottom, 0.0, pltpu.roll(here, LEVELS - 1, 0))
-            beside = ref[s, x - 1, :, columns_of(t)] + ref[s, x + 1, :, columns_of(t)]
-            beside = (beside + (above + below)) + (left + right)
+            beside = (above + below) + (left + right)
+            for side in sides:
+                beside = beside + ref[s, side, :, columns_of(t)]
             yield here, beside - 6.0 * here
             before, here, right_of = shifted, following, right_next
 
@@ -308,35 +332,35 @@
     def rows_of(x, t):
         return pl.ds(pl.multiple_of(((x - 1) * TILES + t) * LEVELS, LEVELS), LEVELS)
 
-    def first_step(s, x):
+    def first_step(s, x, sides, new_wave, new_adj):
         at = source_of(s) - (x - 1) * (TILES * LEVELS * LANES)
-        wavelet = source_wave[s, 0]
-        both = zip(laplace(wave0, s, x), laplace(adj0, s, x), strict=True)
-        for t, ((wave, wave_lap), (adj, adj_lap)) in enumerate(both):
+        wavelet = source_wave[0, s]
+        pair = zip(laplace(wave0, s, x, sides), laplace(adj0, s, x, sides), strict=True)
+        for t, ((wave, wave_lap), (adj, adj_lap)) in enumerate(pair):
             cols = columns_of(t)
             v = vel[x - 1, :, cols]
             pushed = v * wave_lap + jnp.where(place == at - t * (LEVELS * LANES), wavelet, 0.0)
-            wave1[s, x, :, cols] = (2.0 * wave - prev[s, x - 1, :, cols]) + pushed
+            new_wave[:, cols] = (2.0 * wave - prev[s, x - 1, :, cols]) + pushed
             prev[s, x - 1, :, cols] = pushed
             drawn = injected[s, rows_of(x, t), pl.ds(0, LANES)]
-            adj1[s, x, :, cols] = (2.0 * adj - after[s, x - 1, :, cols]) + (v * adj_lap + drawn)
-
-    def second_step(s, x, total, place_x, first):
+            new_adj[:, cols] = (2.0 * adj - after[s, x - 1, :, cols]) + (v * adj_lap + drawn)
+
+    def second_step(s, x, total, place_x):
         at = source_of(s) - (x - 1) * (TILES * LEVELS * LANES)
-        wavelet = source_wave[s, 1]
+        wavelet = source_wave[1, s]
         inside = aperture[s, 0] == dom
         for k in range(1, 8):
             inside = inside | (aperture[s, k] == dom)
         weight = jnp.where(inside, scale, 0.0)
-        both = zip(laplace(wave1, s, x), laplace(adj1, s, x), strict=True)
-        for t, ((_, wave_lap), (adj, adj_lap)) in enumerate(both):
+        pair = zip(laplace(wave1, s, x), laplace(adj1, s, x), strict=True)
+        for t, ((_, wave_lap), (adj, adj_lap)) in enumerate(pair):
             cols = columns_of(t)
             v = vel[x - 1, :, cols]
             pushed = v * wave_lap + jnp.where(place == at - t * (LEVELS * LANES), wavelet, 0.0)
             drawn = injected[s, rows_of(x, t), pl.ds(LANES, LANES)]
             zero = (2.0 * adj - adj0[s, x, :, cols]) + (v * adj_lap + drawn)
             image = weight * (adj * pushed + zero * prev[s, x - 1, :, cols])
-            total[place_x, :, cols] = image if first else total[place_x, :, cols] + image
+            total[place_x, :, cols] += image
 
     def inject(s):
         local = cells_ref[pl.ds(s, 1), :] - dom * CELLS
@@ -370,29 +394,63 @@
 
         lax.fori_loop(first, last, step, 0)
 
-    vel_load.wait()
-
-    def inner_first(s):
+    def end_plane(way):
+        return 1 + (1 - way) * (PLANES - 1)
+
+    def ghost_plane(way):
+        return (1 - way) * (PLANES + 1)
+
+    for copy in small_loads:
+        copy.wait()
+
+    def phase_one(s):
+        advance(0, s)
         inject(s)
         for copy in load(s):
             copy.wait()
-        planes(2, PLANES, lambda x: first_step(s, x))
-
-    each_shot(inner_first)
+
+        def part(way):
+            x = end_plane(way)
+            first_step(s, x, (2 + (1 - way) * (PLANES - 3),), ends.at[way, 0, s], ends.at[way, 1, s])
+
+        planes(0, 2, part)
+        send_first_legs(2, s)
+        send_first_legs(3, s)
+
+    each_shot(phase_one)
+
+    def phase_two(s):
+        advance(1, s)
+
+        def plane(x):
+            first_step(s, x, (x - 1, x + 1), wave1.at[s, x], adj1.at[s, x])
+
+        planes(2, PLANES, plane)
+
+    each_shot(phase_two)
 
     def clear_inner(x):
         inner[x] = jnp.zeros((LEVELS, COLUMNS), jnp.float32)
 
     planes(0, PLANES - 2, clear_inner)
 
-    def ends_first(s):
-        pass_on(0, s)
-        take_layers(0, s)
-        planes(0, 2, lambda k: first_step(s, 1 + k * (PLANES - 1)))
-        send_layers(1, s)
-        planes(2, PLANES, lambda x: second_step(s, x, inner, x - 2, False))
-
-    each_shot(ends_first)
+    def phase_three(s):
+        advance(2, s)
+        take_layer(0, s)
+        take_layer(1, s)
+
+        def complete(way):
+            x, ghost = end_plane(way), ghost_plane(way)
+            v = vel[x - 1]
+            pushed = v * wave0[s, ghost]
+            wave1[s, x] = ends[way, 0, s] + pushed
+            prev[s, x - 1] += pushed
+            adj1[s, x] = ends[way, 1, s] + v * adj0[s, ghost]
+
+        planes(0, 2, complete)
+        planes(2, PLANES, lambda x: second_step(s, x, inner, x - 2))
+
+    each_shot(phase_three)
 
     def eighth_of(index):
         return pl.ds(pl.multiple_of(index * EIGHTH, EIGHTH), EIGHTH)
@@ -433,36 +491,51 @@
     planes(0, 2, clear_edge)
 
     def ends_second(s):
-        pass_on(1, s)
-        take_layers(1, s)
-        planes(0, 2, lambda k: second_step(s, 1 + k * (PLANES - 1), edge, k, False))
-
-    ends_second(0)
-
-    inner_part[...] = inner[:, :, eighth_of(eighth)]
+        take_layer(2, s)
+        take_layer(3, s)
+
+        def part(way):
+            x, ghost = end_plane(way), ghost_plane(way)
+            v = vel_ghost[1 - way]
+            wave1[s, ghost] += v * wave0[s, x]
+            adj1[s, ghost] += v * adj0[s, x]
+            second_step(s, x, edge, 1 - way)
+
+        planes(0, 2, part)
+
+    def swap():
+        return remote(
+            inner_part,
+            pair_got,
+            pair_sem.at[0],
+            pair_sem.at[1],
+            {"shot": shot + 2 - 4 * lower},
+        )
 
     def add_inner(k):
         scatter(k).wait_recv()
         inner_part[...] += inner_got[k]
 
-    every(8, add_inner)
-    swap = remote(
-        inner_part,
-        pair_got,
-        pair_sem.at[0],
-        pair_sem.at[1],
-        {"shot": shot + 2 - 4 * lower},
-    )
-    swap.start()
-
-    ends_second(1)
-
-    swap.wait_recv()
-    out_ref[pl.ds(1, PLANES - 2), :, eighth_of(eighth)] = inner_part[...] + pair_got[...]
-    every(8, lambda k: gather(k).start())
-
-    ends_second(2)
-    ends_second(3)
+    def sum_inner():
+        inner_part[...] = inner[:, :, eighth_of(eighth)]
+        every(8, add_inner)
+        swap().start()
+
+    def share_inner():
+        swap().wait_recv()
+        out_ref[pl.ds(1, PLANES - 2), :, eighth_of(eighth)] = inner_part[...] + pair_got[...]
+        every(8, lambda k: gather(k).start())
+
+    when_each(from_has, lambda way: vel_layer(way).wait_recv())
+
+    def phase_four(s, carry):
+        pl.when(s < SHOTS)(lambda: advance(3, s))
+        pl.when(s == 2)(sum_inner)
+        pl.when(s == 4)(share_inner)
+        pl.when(s >= 2)(lambda: ends_second(s - 2))
+        return carry
+
+    lax.fori_loop(0, SHOTS + 2, phase_four, 0)
 
     def lane_tile(index):
         return pl.ds(pl.multiple_of(index * LANES, LANES), LANES)
@@ -497,9 +570,10 @@
     edge_out[:, :, lane_tile(shot)] = lax.fori_loop(1, GROUP, add_edge, edge[:, :, lane_tile(shot)])
     every(GROUP, lambda k: spread(k).start())
 
-    for step in (0, 1):
-        each_shot(functools.partial(end_sends, step))
-    swap.wait_send()
+    for k in range(4):
+        each_shot(functools.partial(end_legs, k))
+    when_each(has, lambda way: vel_layer(way).wait_send())
+    swap().wait_send()
     every(8, lambda k: scatter(k).wait_send())
     every(8, lambda k: gather(k).wait_send())
     every(8, lambda k: gathered(k).wait_recv())
@@ -511,19 +585,23 @@
 
 
 def body(*arguments):
+    arguments = (*arguments[:6], arguments[6].T, *arguments[7:])
     scale = float(lax.axis_size("shot") * SHOTS) ** (-0.5)
     f32 = jnp.float32
     block = (LEVELS, COLUMNS)
     dma = pltpu.SemaphoreType.DMA
     hbm = pl.BlockSpec(memory_space=pltpu.HBM)
-    vmem = pl.BlockSpec(memory_space=pltpu.VMEM)
-    smem = pl.BlockSpec(memory_space=pltpu.SMEM)
     return pl.pallas_call(
         functools.partial(kernel, scale),
         out_shape=jax.ShapeDtypeStruct((PLANES, *block), f32),
-        in_specs=[hbm, hbm, hbm, hbm, hbm, smem, smem, vmem, vmem, smem],
-        out_specs=vmem,
+        in_specs=[hbm] * 10,
+        out_specs=pl.BlockSpec(memory_space=pltpu.VMEM),
         scratch_shapes=[
+            pltpu.SMEM((SHOTS,), jnp.int32),
+            pltpu.SMEM((2, SHOTS), f32),
+            pltpu.VMEM((SHOTS, RECEIVERS), jnp.int32),
+            pltpu.VMEM((SHOTS, 2, RECEIVERS), f32),
+            pltpu.SMEM((SHOTS, 8), jnp.int32),
             pltpu.VMEM((PLANES, *block), f32),
             pltpu.VMEM((SHOTS, PLANES + 2, *block), f32),
             pltpu.VMEM((SHOTS, PLANES + 2, *block), f32),
@@ -535,13 +613,17 @@
             pltpu.VMEM((PLANES - 2, *block), f32),
             pltpu.VMEM((2, *block), f32),
             pltpu.VMEM((2, *block), f32),
+            pltpu.VMEM((2, 2, SHOTS, *block), f32),
+            pltpu.VMEM((2, *block), f32),
             pltpu.VMEM((4, SHOTS, LEVELS, HALF), f32),
             pltpu.VMEM((8, PLANES - 2, LEVELS, EIGHTH), f32),
             pltpu.VMEM((PLANES - 2, LEVELS, EIGHTH), f32),
             pltpu.VMEM((PLANES - 2, LEVELS, EIGHTH), f32),
             pltpu.VMEM((GROUP, 2, LEVELS, LANES), f32),
             dma((SHOTS, 4)),
-            dma,
+            dma((6,)),
+            dma((2,)),
+            dma((2,)),
             dma((2, 4, SHOTS)),
             dma((2, 4, SHOTS)),
             dma((2, 4, SHOTS)),
@@ -557,7 +639,7 @@
             dma((GROUP,)),
         ],
         compiler_params=pltpu.CompilerParams(
-            collective_id=0, has_side_effects=True, vmem_limit_bytes=48 * 2**20
+            collective_id=0, has_side_effects=True, vmem_limit_bytes=64 * 2**20
         ),
         name="gradient",
     )(*arguments)

time: 74.5 us -> 58.9 us (0.79)
  the two profiles are of different devices: /device:TPU:7 before, /device:TPU:65 now
where the time goes in v2:
time: 58.9 us; the launch traced here: 58.8 us
  Pallas kernels  56.9 us (97%)
  local copies, waits for them, and re-layouts  1.87 us (3%)
    pallas_call x1, Pallas kernels, body(): pl.pallas_call(functools.partial(kernel, scale), out_shape=jax.ShapeDtype...  56.9 us
    unnamed x1, local copies, waits for them, and re-layouts  1.87 us

profile of v2, /device:TPU:65, one launch (start us, length us, event | category | flops | bytes accessed | tf_op | source)
XLA Modules:
  0.0 58.8 jit_solution(369748884896304666)
XLA Ops:
  0.0 56.9 %gradient.1 = f32[8,8,2048]{2,1,0:T(8,128)} custom-call(f32[8,8,2048]{2,1,0:T(8,128)} %vel_hbm.1, f32[4,8,8,2048]{3,2,1,0:T(8,128)} %wave_prev_hbm.1, f32[4,8,8,2048]{3,2,1,0:T(8,128)} %wave_now_hbm.1, f32[4,8,8,2048]{3,2,1,0:T(8,128)} %adj_next_hbm.1, f32[4,8,8,2048]{3,2,1,0:T(8,128)} %adj_now_hbm.1, s32[4]{0:T(128)} %source_cell_hbm.1, f32[2,4]{1,0:T(2,128)} %bitcast.1, ...), custom_call_target="tpu_custom_call" | custom-call | tf_op jit(solution)/shard_map/gradient/pallas_call | solution.py:594
  56.9 1.9 %copy.12 = f32[8,8,2048]{2,1,0:T(8,128)} copy(f32[8,8,2048]{2,1,0:T(8,128)} %gradient.1) | data formatting | bytes 1048576

commit v3 on v2

--- a/solution.py
+++ b/solution.py
@@ -19,6 +19,8 @@
 HALF = COLUMNS // 2
 CELLS = PLANES * LEVELS * COLUMNS
 EIGHTH = COLUMNS // 8
+MIDDLE = PLANES - 4
+WINDOW = 2
 UP, DOWN = 0, 1
 ENDS = (PLANES, 1)
 GHOSTS = (0, PLANES + 1)
@@ -51,19 +53,26 @@
     after,
     injected,
     inner,
-    edge,
-    edge_out,
+    beside,
+    beside_out,
+    outer,
+    outer_got,
+    outer_out,
     ends,
     vel_ghost,
     relay_buf,
     inner_got,
     inner_part,
-    pair_got,
-    edge_got,
+    inner_pair,
+    beside_got,
+    beside_part,
+    beside_pair,
     load_sem,
     small_sem,
     vel_send,
     vel_recv,
+    share_send,
+    share_recv,
     send_sem,
     recv_sem,
     relay_send,
@@ -73,8 +82,8 @@
     pair_sem,
     gather_send,
     gather_recv,
-    edge_send,
-    edge_recv,
+    outer_send,
+    outer_recv,
     spread_send,
     spread_recv,
 ):
@@ -236,9 +245,9 @@
     def advance(k, s):
         when_each(far, lambda way: direct(k, s, way).wait_send())
         when_each(near, lambda way: whole(k, s, way).wait_send())
-        pl.when(s < SHOTS - 2)(lambda: send_layer(k, s + 2))
+        pl.when(s < SHOTS - WINDOW)(lambda: send_layer(k, s + WINDOW))
         if k < 3:
-            pl.when(s >= SHOTS - 2)(lambda: send_layer(k + 1, s + 2 - SHOTS))
+            pl.when(s >= SHOTS - WINDOW)(lambda: send_layer(k + 1, s + WINDOW - SHOTS))
 
         def pass_on(way):
             leg_one(k, s, way).wait_recv()
@@ -258,14 +267,29 @@
         when_each(far, lambda way: leg_one(k, s, way).wait_send())
         when_each(relays, lambda way: leg_two(k, s, way).wait_send())
 
-    def vel_layer(way):
-        return remote(
-            vel_hbm.at[ENDS[way] - 1],
-            vel_ghost.at[way],
+    def eighth_of(index):
+        return pl.ds(pl.multiple_of(index * EIGHTH, EIGHTH), EIGHTH)
+
+    def vel_piece(way):
+        return remote(
+            vel_hbm.at[ENDS[way] - 1, :, eighth_of(eighth)],
+            vel_ghost.at[way, :, eighth_of(eighth)],
             vel_send.at[way],
             vel_recv.at[way],
             towards[way],
         )
+
+    def share_vel(k):
+        mine = vel_ghost.at[:, :, eighth_of(eighth)]
+        peer = member(lax.rem(eighth + k, 8))
+        return remote(mine, mine, share_send.at[k], share_recv.at[k], peer)
+
+    def shared_vel(k):
+        peer = lax.rem(eighth - k + 8, 8)
+        there = vel_ghost.at[:, :, eighth_of(peer)]
+        return remote(there, there, share_send.at[k], share_recv.at[k], member(peer))
+
+    eighths = range(1, 8)
 
     def each_shot(body):
         def step(s, carry):
@@ -276,13 +300,13 @@
 
     for k in (0, 1):
         each_shot(functools.partial(send_first_legs, k))
-    when_each(has, lambda way: vel_layer(way).start())
-    send_layer(0, 0)
-    send_layer(0, 1)
+    when_each(has, lambda way: vel_piece(way).start())
+    for s in range(WINDOW):
+        send_layer(0, s)
 
     def clear_ghosts(way):
         nothing = jnp.zeros((LEVELS, COLUMNS), jnp.float32)
-        vel_ghost[way] = nothing
+        vel_ghost[way, :, eighth_of(eighth)] = jnp.zeros((LEVELS, EIGHTH), jnp.float32)
 
         def clear(s):
             for block in (wave0, adj0, wave1, adj1):
@@ -345,7 +369,7 @@
             drawn = injected[s, rows_of(x, t), pl.ds(0, LANES)]
             new_adj[:, cols] = (2.0 * adj - after[s, x - 1, :, cols]) + (v * adj_lap + drawn)
 
-    def second_step(s, x, total, place_x):
+    def second_step(s, x, add):
         at = source_of(s) - (x - 1) * (TILES * LEVELS * LANES)
         wavelet = source_wave[1, s]
         inside = aperture[s, 0] == dom
@@ -360,7 +384,7 @@
             drawn = injected[s, rows_of(x, t), pl.ds(LANES, LANES)]
             zero = (2.0 * adj - adj0[s, x, :, cols]) + (v * adj_lap + drawn)
             image = weight * (adj * pushed + zero * prev[s, x - 1, :, cols])
-            total[place_x, :, cols] += image
+            add(t, image)
 
     def inject(s):
         local = cells_ref[pl.ds(s, 1), :] - dom * CELLS
@@ -419,6 +443,22 @@
 
     each_shot(phase_one)
 
+    def clear_inner(x):
+        inner[x] = jnp.zeros((LEVELS, COLUMNS), jnp.float32)
+
+    def clear_outer(t):
+        outer[t] = jnp.zeros((2, LEVELS, LANES), jnp.float32)
+
+    def clear_beside(way):
+        beside[way] = jnp.zeros((LEVELS, COLUMNS), jnp.float32)
+
+    planes(0, MIDDLE, clear_inner)
+    planes(0, 2, clear_beside)
+    planes(0, TILES, clear_outer)
+    when_each(from_has, lambda way: vel_piece(way).wait_recv())
+    for k in eighths:
+        share_vel(k).start()
+
     def phase_two(s):
         advance(1, s)
 
@@ -427,12 +467,129 @@
 
         planes(2, PLANES, plane)
 
+        def middle(x):
+            def add(t, image):
+                inner[x - 3, :, columns_of(t)] += image
+
+            second_step(s, x, add)
+
+        planes(3, PLANES - 1, middle)
+
     each_shot(phase_two)
 
-    def clear_inner(x):
-        inner[x] = jnp.zeros((LEVELS, COLUMNS), jnp.float32)
-
-    planes(0, PLANES - 2, clear_inner)
+    sets = (
+        (inner, inner_got, inner_part, inner_pair, out_ref.at[pl.ds(2, MIDDLE)]),
+        (beside, beside_got, beside_part, beside_pair, beside_out),
+    )
+
+    def scatter(which, k):
+        total, got, _, _, _ = sets[which]
+        peer = lax.rem(eighth + k, 8)
+        return remote(
+            total.at[:, :, eighth_of(peer)],
+            got.at[k],
+            red_send.at[which, k],
+            red_recv.at[which, k],
+            member(peer),
+        )
+
+    def swap(which):
+        _, _, part, pair, _ = sets[which]
+        return remote(
+            part,
+            pair,
+            pair_sem.at[which, 0],
+            pair_sem.at[which, 1],
+            {"shot": shot + 2 - 4 * lower},
+        )
+
+    def gather(which, k):
+        mine = sets[which][4].at[:, :, eighth_of(eighth)]
+        return remote(
+            mine,
+            mine,
+            gather_send.at[which, k],
+            gather_recv.at[which, k],
+            member(lax.rem(eighth + k, 8)),
+        )
+
+    def gathered(which, k):
+        peer = lax.rem(eighth - k + 8, 8)
+        there = sets[which][4].at[:, :, eighth_of(peer)]
+        return remote(
+            there, there, gather_send.at[which, k], gather_recv.at[which, k], member(peer)
+        )
+
+    def start_sum(which):
+        for k in eighths:
+            scatter(which, k).start()
+
+    def add_up(which):
+        total, got, part, _, _ = sets[which]
+        value = total[:, :, eighth_of(eighth)]
+        for k in eighths:
+            scatter(which, k).wait_recv()
+            value = value + got[k]
+        part[...] = value
+        swap(which).start()
+
+    def give_back(which):
+        _, _, part, pair, result = sets[which]
+        swap(which).wait_recv()
+        result[:, :, eighth_of(eighth)] = part[...] + pair[...]
+        for k in eighths:
+            gather(which, k).start()
+
+    def end_sum(which):
+        swap(which).wait_send()
+        for k in eighths:
+            scatter(which, k).wait_send()
+            gather(which, k).wait_send()
+            gathered(which, k).wait_recv()
+
+    def scatter_outer(k):
+        peer = lax.rem(shot + k, GROUP)
+        return remote(
+            outer.at[peer], outer_got.at[k], outer_send.at[k], outer_recv.at[k], {"shot": peer}
+        )
+
+    def spread(k):
+        mine = outer_out.at[shot]
+        return remote(
+            mine, mine, spread_send.at[k], spread_recv.at[k], {"shot": lax.rem(shot + k, GROUP)}
+        )
+
+    def spread_from(k):
+        peer = lax.rem(shot - k + GROUP, GROUP)
+        there = outer_out.at[peer]
+        return remote(there, there, spread_send.at[k], spread_recv.at[k], {"shot": peer})
+
+    peers = range(1, GROUP)
+
+    def start_outer():
+        for k in peers:
+            scatter_outer(k).start()
+
+    def sum_outer():
+        total = outer[shot]
+        for k in peers:
+            scatter_outer(k).wait_recv()
+            total = total + outer_got[k]
+        outer_out[shot] = total
+        for k in peers:
+            spread(k).start()
+
+    def end_outer():
+        for k in peers:
+            scatter_outer(k).wait_send()
+            spread(k).wait_send()
+        for k in peers:
+            spread_from(k).wait_recv()
+        for t in range(TILES):
+            for side in (0, 1):
+                out_ref[side * (PLANES - 1), :, columns_of(t)] = outer_out[t, side]
+
+    start_sum(0)
 
     def phase_three(s):
         advance(2, s)
@@ -448,47 +605,17 @@
             adj1[s, x] = ends[way, 1, s] + v * adj0[s, ghost]
 
         planes(0, 2, complete)
-        planes(2, PLANES, lambda x: second_step(s, x, inner, x - 2))
+
+        def next_to(way):
+            def add(t, image):
+                beside[1 - way, :, columns_of(t)] += image
+
+            second_step(s, 2 + (1 - way) * (PLANES - 3), add)
+
+        planes(0, 2, next_to)
 
     each_shot(phase_three)
-
-    def eighth_of(index):
-        return pl.ds(pl.multiple_of(index * EIGHTH, EIGHTH), EIGHTH)
-
-    def scatter(k):
-        peer = lax.rem(eighth + k, 8)
-        return remote(
-            inner.at[:, :, eighth_of(peer)],
-            inner_got.at[k],
-            red_send.at[k],
-            red_recv.at[k],
-            member(peer),
-        )
-
-    def gather(k):
-        mine = out_ref.at[pl.ds(1, PLANES - 2), :, eighth_of(eighth)]
-        return remote(
-            mine, mine, gather_send.at[k], gather_recv.at[k], member(lax.rem(eighth + k, 8))
-        )
-
-    def gathered(k):
-        peer = lax.rem(eighth - k + 8, 8)
-        there = out_ref.at[pl.ds(1, PLANES - 2), :, eighth_of(peer)]
-        return remote(there, there, gather_send.at[k], gather_recv.at[k], member(peer))
-
-    def every(count, body):
-        def step(k, carry):
-            body(k)
-            return carry
-
-        lax.fori_loop(1, count, step, 0)
-
-    every(8, lambda k: scatter(k).start())
-
-    def clear_edge(x):
-        edge[x] = jnp.zeros((LEVELS, COLUMNS), jnp.float32)
-
-    planes(0, 2, clear_edge)
+    start_sum(1)
 
     def ends_second(s):
         take_layer(2, s)
@@ -499,89 +626,39 @@
             v = vel_ghost[1 - way]
             wave1[s, ghost] += v * wave0[s, x]
             adj1[s, ghost] += v * adj0[s, x]
-            second_step(s, x, edge, 1 - way)
+
+            def add(t, image):
+                outer[t, 1 - way] += image
+
+            second_step(s, x, add)
 
         planes(0, 2, part)
 
-    def swap():
-        return remote(
-            inner_part,
-            pair_got,
-            pair_sem.at[0],
-            pair_sem.at[1],
-            {"shot": shot + 2 - 4 * lower},
-        )
-
-    def add_inner(k):
-        scatter(k).wait_recv()
-        inner_part[...] += inner_got[k]
-
-    def sum_inner():
-        inner_part[...] = inner[:, :, eighth_of(eighth)]
-        every(8, add_inner)
-        swap().start()
-
-    def share_inner():
-        swap().wait_recv()
-        out_ref[pl.ds(1, PLANES - 2), :, eighth_of(eighth)] = inner_part[...] + pair_got[...]
-        every(8, lambda k: gather(k).start())
-
-    when_each(from_has, lambda way: vel_layer(way).wait_recv())
-
-    def phase_four(s, carry):
-        pl.when(s < SHOTS)(lambda: advance(3, s))
-        pl.when(s == 2)(sum_inner)
-        pl.when(s == 4)(share_inner)
-        pl.when(s >= 2)(lambda: ends_second(s - 2))
-        return carry
-
-    lax.fori_loop(0, SHOTS + 2, phase_four, 0)
-
-    def lane_tile(index):
-        return pl.ds(pl.multiple_of(index * LANES, LANES), LANES)
-
-    def scatter_edge(k):
-        peer = lax.rem(shot + k, GROUP)
-        return remote(
-            edge.at[:, :, lane_tile(peer)],
-            edge_got.at[k],
-            edge_send.at[k],
-            edge_recv.at[k],
-            {"shot": peer},
-        )
-
-    def spread(k):
-        mine = edge_out.at[:, :, lane_tile(shot)]
-        return remote(
-            mine, mine, spread_send.at[k], spread_recv.at[k], {"shot": lax.rem(shot + k, GROUP)}
-        )
-
-    def spread_from(k):
-        peer = lax.rem(shot - k + GROUP, GROUP)
-        there = edge_out.at[:, :, lane_tile(peer)]
-        return remote(there, there, spread_send.at[k], spread_recv.at[k], {"shot": peer})
-
-    every(GROUP, lambda k: scatter_edge(k).start())
-
-    def add_edge(k, carry):
-        scatter_edge(k).wait_recv()
-        return carry + edge_got[k]
-
-    edge_out[:, :, lane_tile(shot)] = lax.fori_loop(1, GROUP, add_edge, edge[:, :, lane_tile(shot)])
-    every(GROUP, lambda k: spread(k).start())
+    advance(3, 0)
+    advance(3, 1)
+    add_up(0)
+    advance(3, 2)
+    advance(3, 3)
+    give_back(0)
+    for k in eighths:
+        shared_vel(k).wait_recv()
+    add_up(1)
+
+    each_shot(ends_second)
+    start_outer()
+    give_back(1)
+    end_sum(0)
+    sum_outer()
+    end_sum(1)
+    out_ref[1] = beside_out[0]
+    out_ref[PLANES - 2] = beside_out[1]
 
     for k in range(4):
         each_shot(functools.partial(end_legs, k))
-    when_each(has, lambda way: vel_layer(way).wait_send())
-    swap().wait_send()
-    every(8, lambda k: scatter(k).wait_send())
-    every(8, lambda k: gather(k).wait_send())
-    every(8, lambda k: gathered(k).wait_recv())
-    every(GROUP, lambda k: scatter_edge(k).wait_send())
-    every(GROUP, lambda k: spread(k).wait_send())
-    every(GROUP, lambda k: spread_from(k).wait_recv())
-    out_ref[0] = edge_out[0]
-    out_ref[PLANES - 1] = edge_out[1]
+    when_each(has, lambda way: vel_piece(way).wait_send())
+    for k in eighths:
+        share_vel(k).wait_send()
+    end_outer()
 
 
 def body(*arguments):
@@ -610,29 +687,36 @@
             pltpu.VMEM((SHOTS, PLANES, *block), f32),
             pltpu.VMEM((SHOTS, PLANES, *block), f32),
             pltpu.VMEM((SHOTS, CELLS // LANES, 2 * LANES), f32),
-            pltpu.VMEM((PLANES - 2, *block), f32),
+            pltpu.VMEM((MIDDLE, *block), f32),
             pltpu.VMEM((2, *block), f32),
             pltpu.VMEM((2, *block), f32),
+            pltpu.VMEM((TILES, 2, LEVELS, LANES), f32),
+            pltpu.VMEM((TILES, 2, LEVELS, LANES), f32),
+            pltpu.VMEM((TILES, 2, LEVELS, LANES), f32),
             pltpu.VMEM((2, 2, SHOTS, *block), f32),
             pltpu.VMEM((2, *block), f32),
             pltpu.VMEM((4, SHOTS, LEVELS, HALF), f32),
-            pltpu.VMEM((8, PLANES - 2, LEVELS, EIGHTH), f32),
-            pltpu.VMEM((PLANES - 2, LEVELS, EIGHTH), f32),
-            pltpu.VMEM((PLANES - 2, LEVELS, EIGHTH), f32),
-            pltpu.VMEM((GROUP, 2, LEVELS, LANES), f32),
+            pltpu.VMEM((8, MIDDLE, LEVELS, EIGHTH), f32),
+            pltpu.VMEM((MIDDLE, LEVELS, EIGHTH), f32),
+            pltpu.VMEM((MIDDLE, LEVELS, EIGHTH), f32),
+            pltpu.VMEM((8, 2, LEVELS, EIGHTH), f32),
+            pltpu.VMEM((2, LEVELS, EIGHTH), f32),
+            pltpu.VMEM((2, LEVELS, EIGHTH), f32),
             dma((SHOTS, 4)),
             dma((6,)),
             dma((2,)),
             dma((2,)),
+            dma((8,)),
+            dma((8,)),
             dma((2, 4, SHOTS)),
             dma((2, 4, SHOTS)),
             dma((2, 4, SHOTS)),
             dma((2, 4, SHOTS)),
-            dma((8,)),
-            dma((8,)),
-            dma((2,)),
-            dma((8,)),
-            dma((8,)),
+            dma((2, 8)),
+            dma((2, 8)),
+            dma((2, 2)),
+            dma((2, 8)),
+            dma((2, 8)),
             dma((GROUP,)),
             dma((GROUP,)),
             dma((GROUP,)),

time: 58.9 us -> 53.1 us (0.902)
  Pallas kernels: 56.9 us -> 51.1 us
    pallas_call x1, Pallas kernels: 56.9 us -> 51.1 us  [body(): pl.pallas_call(functools.partial(kernel, scale), out_shape=jax.ShapeDtype...]
where the time goes in v3:
time: 53.1 us; the launch traced here: 53 us
  Pallas kernels  51.1 us (96%)
  local copies, waits for them, and re-layouts  1.87 us (4%)
    pallas_call x1, Pallas kernels, body(): pl.pallas_call(functools.partial(kernel, scale), out_shape=jax.ShapeDtype...  51.1 us
    unnamed x1, local copies, waits for them, and re-layouts  1.87 us

profile of v3, /device:TPU:65, one launch (start us, length us, event | category | flops | bytes accessed | tf_op | source)
XLA Modules:
  0.0 53.0 jit_solution(16166952559463305319)
XLA Ops:
  0.0 51.1 %gradient.1 = f32[8,8,2048]{2,1,0:T(8,128)} custom-call(f32[8,8,2048]{2,1,0:T(8,128)} %vel_hbm.1, f32[4,8,8,2048]{3,2,1,0:T(8,128)} %wave_prev_hbm.1, f32[4,8,8,2048]{3,2,1,0:T(8,128)} %wave_now_hbm.1, f32[4,8,8,2048]{3,2,1,0:T(8,128)} %adj_next_hbm.1, f32[4,8,8,2048]{3,2,1,0:T(8,128)} %adj_now_hbm.1, s32[4]{0:T(128)} %source_cell_hbm.1, f32[2,4]{1,0:T(2,128)} %bitcast.1, ...), custom_call_target="tpu_custom_call" | custom-call | tf_op jit(solution)/shard_map/gradient/pallas_call | solution.py:671
  51.1 1.9 %copy.12 = f32[8,8,2048]{2,1,0:T(8,128)} copy(f32[8,8,2048]{2,1,0:T(8,128)} %gradient.1) | data formatting | bytes 1048576

commit v4 on v3

--- a/solution.py
+++ b/solution.py
@@ -670,7 +670,7 @@
     hbm = pl.BlockSpec(memory_space=pltpu.HBM)
     return pl.pallas_call(
         functools.partial(kernel, scale),
-        out_shape=jax.ShapeDtypeStruct((PLANES, *block), f32),
+        out_shape=pltpu.VMEM((PLANES, *block), f32),
         in_specs=[hbm] * 10,
         out_specs=pl.BlockSpec(memory_space=pltpu.VMEM),
         scratch_shapes=[
@@ -723,7 +723,7 @@
             dma((GROUP,)),
         ],
         compiler_params=pltpu.CompilerParams(
-            collective_id=0, has_side_effects=True, vmem_limit_bytes=64 * 2**20
+            collective_id=0, has_side_effects=True, vmem_limit_bytes=60 * 2**20
         ),
         name="gradient",
     )(*arguments)

time: 53.1 us -> 51 us (0.960)
  local copies, waits for them, and re-layouts: 1.87 us -> 0.8 us
  Pallas kernels: 51.1 us -> 50.2 us
    unnamed x1, local copies, waits for them, and re-layouts: 1.87 us -> 0.8 us
    pallas_call x1, Pallas kernels: 51.1 us -> 50.2 us  [body(): pl.pallas_call(functools.partial(kernel, scale), out_shape=pltpu.VMEM((PL...]
where the time goes in v4:
time: 51 us
  Pallas kernels  50.2 us (98%)
  local copies, waits for them, and re-layouts  0.8 us (2%)
    pallas_call x1, Pallas kernels, body(): pl.pallas_call(functools.partial(kernel, scale), out_shape=pltpu.VMEM((PL...  50.2 us

profile of v4, /device:TPU:65, one launch (start us, length us, event | category | flops | bytes accessed | tf_op | source)
XLA Modules:
  0.0 51.0 jit_solution(7883356528258696780)
XLA Ops:
  0.0 50.2 %gradient.1 = f32[8,8,2048]{2,1,0:T(8,128)S(1)} custom-call(f32[8,8,2048]{2,1,0:T(8,128)} %vel_hbm.1, f32[4,8,8,2048]{3,2,1,0:T(8,128)} %wave_prev_hbm.1, f32[4,8,8,2048]{3,2,1,0:T(8,128)} %wave_now_hbm.1, f32[4,8,8,2048]{3,2,1,0:T(8,128)} %adj_next_hbm.1, f32[4,8,8,2048]{3,2,1,0:T(8,128)} %adj_now_hbm.1, s32[4]{0:T(128)} %source_cell_hbm.1, ...), custom_call_target="tpu_custom_call" | custom-call | tf_op jit(solution)/shard_map/gradient/pallas_call | solution.py:671
  50.2 0.8 %copy.12 = f32[8,8,2048]{2,1,0:T(8,128)} copy(f32[8,8,2048]{2,1,0:T(8,128)S(1)} %gradient.1) | data formatting | bytes 1048576

commit v5 on v4

--- a/solution.py
+++ b/solution.py
@@ -135,22 +135,11 @@
             )
         )
     ]
-    for copy in small_loads:
-        copy.start()
-    for s in range(SHOTS):
-        for copy in load(s):
-            copy.start()
-
     barrier = pltpu.get_barrier_semaphore()
 
     def greet(device):
         pl.semaphore_signal(barrier, inc=1, device_id=device, device_id_type=MESH)
 
-    def greet_peer(k, carry):
-        greet({"shot": lax.rem(shot + k, GROUP)})
-        return carry
-
-    lax.fori_loop(1, GROUP, greet_peer, 0)
     greet(towards[UP])
     greet(towards[DOWN])
 
@@ -165,6 +154,9 @@
         greet(along_dom(-3))
         greet(along_dom(4))
         greet(along_dom(-4))
+
+    for k in range(1, GROUP):
+        greet({"shot": lax.rem(shot + k, GROUP)})
 
     relaying = (column == 0) | (column == 3)
     pl.semaphore_wait(barrier, GROUP + 1 + jnp.where(relaying, 3, 0))
@@ -303,6 +295,12 @@
     when_each(has, lambda way: vel_piece(way).start())
     for s in range(WINDOW):
         send_layer(0, s)
+
+    for copy in small_loads:
+        copy.start()
+    for s in range(SHOTS):
+        for copy in load(s):
+            copy.start()
 
     def clear_ghosts(way):
         nothing = jnp.zeros((LEVELS, COLUMNS), jnp.float32)
@@ -564,7 +562,7 @@
         there = outer_out.at[peer]
         return remote(there, there, spread_send.at[k], spread_recv.at[k], {"shot": peer})
 
-    peers = range(1, GROUP)
+    peers = sorted(range(1, GROUP), key=lambda k: abs(k - GROUP // 2))
 
     def start_outer():
         for k in peers:
@@ -635,8 +633,8 @@
         planes(0, 2, part)
 
     advance(3, 0)
+    add_up(0)
     advance(3, 1)
-    add_up(0)
     advance(3, 2)
     advance(3, 3)
     give_back(0)
@@ -646,8 +644,8 @@
 
     each_shot(ends_second)
     start_outer()
+    end_sum(0)
     give_back(1)
-    end_sum(0)
     sum_outer()
     end_sum(1)
     out_ref[1] = beside_out[0]

time: 51 us -> 50 us (0.980)
  Pallas kernels: 50.2 us -> 49.1 us
    pallas_call x1, Pallas kernels: 50.2 us -> 49.1 us  [body(): pl.pallas_call(functools.partial(kernel, scale), out_shape=pltpu.VMEM((PL...]
where the time goes in v5:
time: 50 us; the launch traced here: 49.9 us
  Pallas kernels  49.1 us (98%)
  local copies, waits for them, and re-layouts  0.8 us (2%)
    pallas_call x1, Pallas kernels, body(): pl.pallas_call(functools.partial(kernel, scale), out_shape=pltpu.VMEM((PL...  49.1 us

profile of v5, /device:TPU:65, one launch (start us, length us, event | category | flops | bytes accessed | tf_op | source)
XLA Modules:
  0.0 49.9 jit_solution(17241278641627984263)
XLA Ops:
  0.0 49.1 %gradient.1 = f32[8,8,2048]{2,1,0:T(8,128)S(1)} custom-call(f32[8,8,2048]{2,1,0:T(8,128)} %vel_hbm.1, f32[4,8,8,2048]{3,2,1,0:T(8,128)} %wave_prev_hbm.1, f32[4,8,8,2048]{3,2,1,0:T(8,128)} %wave_now_hbm.1, f32[4,8,8,2048]{3,2,1,0:T(8,128)} %adj_next_hbm.1, f32[4,8,8,2048]{3,2,1,0:T(8,128)} %adj_now_hbm.1, s32[4]{0:T(128)} %source_cell_hbm.1, ...), custom_call_target="tpu_custom_call" | custom-call | tf_op jit(solution)/shard_map/gradient/pallas_call | solution.py:669
  49.1 0.8 %copy.12 = f32[8,8,2048]{2,1,0:T(8,128)} copy(f32[8,8,2048]{2,1,0:T(8,128)S(1)} %gradient.1) | data formatting | bytes 1048576

commit v6 on v5

--- a/solution.py
+++ b/solution.py
@@ -281,7 +281,7 @@
         there = vel_ghost.at[:, :, eighth_of(peer)]
         return remote(there, there, share_send.at[k], share_recv.at[k], member(peer))
 
-    eighths = range(1, 8)
+    eighths = sorted(range(1, 8), key=lambda k: abs(k - 4))
 
     def each_shot(body):
         def step(s, carry):

time: 50 us -> 50.2 us (level)
  no operation moved by 1% of the time
where the time goes in v6:
time: 50.2 us; the launch traced here: 49.8 us
  Pallas kernels  49 us (98%)
  local copies, waits for them, and re-layouts  0.8 us (2%)
    pallas_call x1, Pallas kernels, body(): pl.pallas_call(functools.partial(kernel, scale), out_shape=pltpu.VMEM((PL...  49 us

profile of v6, /device:TPU:65, one launch (start us, length us, event | category | flops | bytes accessed | tf_op | source)
XLA Modules:
  0.0 49.8 jit_solution(7445496295524524998)
XLA Ops:
  0.0 49.0 %gradient.1 = f32[8,8,2048]{2,1,0:T(8,128)S(1)} custom-call(f32[8,8,2048]{2,1,0:T(8,128)} %vel_hbm.1, f32[4,8,8,2048]{3,2,1,0:T(8,128)} %wave_prev_hbm.1, f32[4,8,8,2048]{3,2,1,0:T(8,128)} %wave_now_hbm.1, f32[4,8,8,2048]{3,2,1,0:T(8,128)} %adj_next_hbm.1, f32[4,8,8,2048]{3,2,1,0:T(8,128)} %adj_now_hbm.1, s32[4]{0:T(128)} %source_cell_hbm.1, ...), custom_call_target="tpu_custom_call" | custom-call | tf_op jit(solution)/shard_map/gradient/pallas_call | solution.py:669
  49.0 0.8 %copy.12 = f32[8,8,2048]{2,1,0:T(8,128)} copy(f32[8,8,2048]{2,1,0:T(8,128)S(1)} %gradient.1) | data formatting | bytes 1048576
